TPU v7x, 32 devices: a whole 2x2x4 slice. The times are simulated.
32 devices in a mesh: rows: 8 (over z, y), blk: 4 (over x, core).
Axes of the slice: x: 2, y: 2, z: 4, core: 2. Of those that a mesh axis runs over, the one named last changes fastest.
Arguments:
- inputs: bfloat16 [8, 1792, 768], P('rows', 'blk'), may hold values from -6 to 6
- encoded: bfloat16 [8, 1536, 768], P('rows', 'blk'), may hold values from -6 to 6
- cotangent: bfloat16 [8, 1792, 768], P('rows', 'blk'), may hold values from -6 to 6
- dec_seg: int32 [8, 1792], P('rows', 'blk'), may hold values from 0 to 2, as said below
- pass_doc: int32 [8, 4], P('rows', 'blk'), may hold values from 0 to 2, as said below
- enc_mask: int32 [8, 1536], P('rows', 'blk'), may hold values from 0 to 1, as said below
- self_query: bfloat16 [768, 768], replicated, may hold values from -0.21875 to 0.21875
- self_key: bfloat16 [768, 768], replicated, may hold values from -0.21875 to 0.21875
- self_value: bfloat16 [768, 768], replicated, may hold values from -0.21875 to 0.21875
- self_output: bfloat16 [768, 768], replicated, may hold values from -3 to 3
- cross_query: bfloat16 [768, 768], replicated, may hold values from -0.21875 to 0.21875
- cross_key: bfloat16 [768, 768], replicated, may hold values from -0.21875 to 0.21875
- cross_value: bfloat16 [768, 768], replicated, may hold values from -0.21875 to 0.21875
- cross_output: bfloat16 [768, 768], replicated, may hold values from -6 to 6
- feed_in: bfloat16 [768, 3072], replicated, may hold values from -0.21875 to 0.21875
- feed_out: bfloat16 [3072, 768], replicated, may hold values from -0.109375 to 0.109375
- gain_self: float32 [768], replicated, may hold values from 0.1 to 1.9
- gain_cross: float32 [768], replicated, may hold values from 0.1 to 1.9
- gain_ff: float32 [768], replicated, may hold values from 0.1 to 1.9
Outputs:
- output: bfloat16 [8, 1792, 768], P('rows', 'blk')
- input_grad: float32 [8, 1792, 768], P('rows', 'blk')
- encoded_grad: float32 [8, 1536, 768], P('rows', 'blk')
- grad_self_query: float32 [768, 768], P('rows', 'blk')
- grad_self_key: float32 [768, 768], P('rows', 'blk')
- grad_self_value: float32 [768, 768], P('rows', 'blk')
- grad_self_output: float32 [768, 768], P('rows', 'blk')
- grad_cross_query: float32 [768, 768], P('rows', 'blk')
- grad_cross_key: float32 [768, 768], P('rows', 'blk')
- grad_cross_value: float32 [768, 768], P('rows', 'blk')
- grad_cross_output: float32 [768, 768], P('rows', 'blk')
- grad_feed_in: float32 [768, 3072], P('rows', 'blk')
- grad_feed_out: float32 [3072, 768], P('rows', 'blk')
- grad_gain_self: float32 [768], P('rows')
- grad_gain_cross: float32 [768], P('rows')
- grad_gain_ff: float32 [768], P('rows')
Inputs may be any that keep to these rules, and one draw needn't show every extreme that they name: `dec_seg`: each row holds three documents of consecutive decoder tokens, numbered 0, 1, 2 in order; document 1 begins within the row's first 448 tokens and ends within its last 448. `pass_doc`: every document of a row is served by one passage or more; the first and the last passage of each row serve document 1. `enc_mask`: the live tokens of each passage are a prefix of 336 to 384 tokens; the first passage of every row is wholly live.
All inputs are finite; a program needn't handle non-finite values.
Results may differ from a plain program's by a relative error of at most 0.025.
Values may be sent and summed in bfloat16 or wider, within the bound.
No kernel may reach another device: no remote copies, remote signals or barrier semaphores. Data moves between devices by JAX's collectives and lax.ppermute only.
A program may use at most 320 MiB of HBM per device.

v0:
```python
import jax
import jax.numpy as jnp
from jax import lax
from jax.sharding import PartitionSpec as P

HEADS = 12
HEAD_DIM = 64
PLEN = 384


NEG_FILL = -1e30
SCALE = 0.125


def split_heads(matrix):
    return matrix.reshape(matrix.shape[0], matrix.shape[1], HEADS, HEAD_DIM)


def join_heads(tensor):
    return jnp.transpose(tensor, (0, 2, 1, 3)).reshape(
        tensor.shape[0], tensor.shape[2], HEADS * HEAD_DIM
    )


def rms_norm(values, gain_vec):
    return values * lax.rsqrt(jnp.mean(values * values, axis=-1, keepdims=True) + 1e-06) * gain_vec


def norm_back(values, gain_vec, grad_out):
    _, pullback = jax.vjp(rms_norm, values, gain_vec)
    return pullback(grad_out)


def project(left, weight):
    return jnp.einsum("rqd,df->rqf", left, weight, preferred_element_type=jnp.float32)


def back_project(grad_out, weight):
    return jnp.einsum("rqf,df->rqd", grad_out, weight, preferred_element_type=jnp.float32)


def weight_grad(left, grad_out):
    return jnp.einsum("rqd,rqf->df", left, grad_out, preferred_element_type=jnp.float32)


def head_scores(queries, keys):
    return (
        jnp.einsum(
            "rqhe,rkhe->rhqk",
            split_heads(queries),
            split_heads(keys),
            preferred_element_type=jnp.float32,
        )
        * SCALE
    )


def empty_state(row_count, query_count):
    return (
        jnp.full((row_count, HEADS, query_count), NEG_FILL, jnp.float32),
        jnp.zeros((row_count, HEADS, query_count), jnp.float32),
        jnp.zeros((row_count, HEADS, query_count, HEAD_DIM), jnp.float32),
    )


def online_block(state, queries, keys, values, allowed):
    run_max, run_sum, run_acc = state
    scores = head_scores(queries, keys)
    allowed = allowed[:, None]
    new_max = jnp.maximum(run_max, jnp.max(jnp.where(allowed, scores, NEG_FILL), axis=-1))
    weights = jnp.where(allowed, jnp.exp(scores - new_max[..., None]), 0.0)
    new_sum = jnp.sum(weights, axis=-1)
    new_acc = jnp.einsum(
        "rhqk,rkhe->rhqe",
        weights.astype(jnp.bfloat16),
        split_heads(values),
        preferred_element_type=jnp.float32,
    )
    return (new_max, new_sum, new_acc)


def finish(state):
    run_max, run_sum, run_acc = state
    return (run_acc / run_sum[..., None], run_max + jnp.log(run_sum))


def grad_pair(queries, grad_ctx, log_sum, delta, keys, values, allowed):
    scores = head_scores(queries, keys)
    probs_now = jnp.where(allowed[:, None], jnp.exp(scores - log_sum[..., None]), 0.0)
    grad_probs = jnp.einsum(
        "rqhe,rkhe->rhqk",
        split_heads(grad_ctx),
        split_heads(values),
        preferred_element_type=jnp.float32,
    )
    grad_scores = (probs_now * (grad_probs - delta[..., None])).astype(jnp.bfloat16)
    grad_query = (
        jnp.einsum(
            "rhqk,rkhe->rqhe", grad_scores, split_heads(keys), preferred_element_type=jnp.float32
        )
        * SCALE
    )
    grad_key = (
        jnp.einsum(
            "rhqk,rqhe->rkhe", grad_scores, split_heads(queries), preferred_element_type=jnp.float32
        )
        * SCALE
    )
    grad_value = jnp.einsum(
        "rhqk,rqhe->rkhe",
        probs_now.astype(jnp.bfloat16),
        split_heads(grad_ctx),
        preferred_element_type=jnp.float32,
    )
    row_count = keys.shape[0]
    key_count = keys.shape[1]
    joined = jnp.concatenate(
        (grad_key.reshape(row_count, key_count, -1), grad_value.reshape(row_count, key_count, -1)),
        axis=-1,
    )
    return (grad_query.reshape(row_count, queries.shape[1], -1), joined)


def head_delta(grad_ctx, attended):
    return jnp.einsum("rqhe,rhqe->rhq", split_heads(grad_ctx).astype(jnp.float32), attended)


def spread_matrix(matrix, row_split, block_count):
    first, second = matrix.shape
    tiles = matrix.reshape(row_split, first // row_split, block_count, second // block_count)
    return jnp.transpose(tiles, (0, 2, 1, 3)).reshape(
        row_split * block_count, first // row_split, second // block_count
    )


def spread_gain(vector, row_split, block_count):
    tiles = vector.reshape(row_split, 1, vector.shape[0] // row_split)
    return jnp.broadcast_to(tiles, (row_split, block_count, vector.shape[0] // row_split)).reshape(
        row_split * block_count, vector.shape[0] // row_split
    )


def local(
    inputs,
    encoded,
    cotangent,
    dec_seg,
    pass_doc,
    enc_mask,
    self_query,
    self_key,
    self_value,
    self_output,
    cross_query,
    cross_key,
    cross_value,
    cross_output,
    feed_in,
    feed_out,
    gain_self,
    gain_cross,
    gain_ff,
):
    row_count, tok_shard, width = inputs.shape
    enc_shard = encoded.shape[1]
    block_count = lax.axis_size("blk")
    row_split = lax.axis_size("rows")
    block_ids = jnp.arange(block_count)
    query_places = lax.axis_index("blk") * tok_shard + jnp.arange(tok_shard)
    start_state = empty_state(row_count, tok_shard)
    residual = inputs.astype(jnp.float32)
    normed_self = rms_norm(residual, gain_self).astype(jnp.bfloat16)
    self_queries = project(normed_self, self_query).astype(jnp.bfloat16)
    self_keys = project(normed_self, self_key).astype(jnp.bfloat16)
    self_values = project(normed_self, self_value).astype(jnp.bfloat16)
    piece_keys = lax.all_gather(self_keys, "blk", axis=1, tiled=True)
    piece_values = lax.all_gather(self_values, "blk", axis=1, tiled=True)
    piece_segs = lax.all_gather(dec_seg, "blk", axis=1, tiled=True)
    key_places = jnp.arange(piece_keys.shape[1])
    allowed = (dec_seg[:, :, None] == piece_segs[:, None, :]) & (
        key_places[None, None, :] <= query_places[None, :, None]
    )
    self_attn, self_lse = finish(
        online_block(start_state, self_queries, piece_keys, piece_values, allowed)
    )
    self_context = join_heads(self_attn).astype(jnp.bfloat16)
    after_self = residual + project(self_context, self_output)
    normed_cross = rms_norm(after_self, gain_cross).astype(jnp.bfloat16)
    cross_queries = project(normed_cross, cross_query).astype(jnp.bfloat16)
    cross_keys = project(encoded, cross_key).astype(jnp.bfloat16)
    cross_values = project(encoded, cross_value).astype(jnp.bfloat16)
    key_docs = jnp.where(enc_mask == 1, jnp.repeat(pass_doc, PLEN, axis=1), -1)
    piece_keys = lax.all_gather(cross_keys, "blk", axis=1, tiled=True)
    piece_values = lax.all_gather(cross_values, "blk", axis=1, tiled=True)
    piece_docs = lax.all_gather(key_docs, "blk", axis=1, tiled=True)
    allowed = dec_seg[:, :, None] == piece_docs[:, None, :]
    cross_attn, cross_lse = finish(
        online_block(start_state, cross_queries, piece_keys, piece_values, allowed)
    )
    cross_context = join_heads(cross_attn).astype(jnp.bfloat16)
    after_cross = after_self + project(cross_context, cross_output)
    normed_ff = rms_norm(after_cross, gain_ff).astype(jnp.bfloat16)
    before_act = project(normed_ff, feed_in)
    hidden = jax.nn.gelu(before_act).astype(jnp.bfloat16)
    output = (after_cross + project(hidden, feed_out)).astype(jnp.bfloat16)
    grad_feed_out = weight_grad(hidden, cotangent)
    grad_hidden = back_project(cotangent, feed_out)
    _, gelu_back = jax.vjp(jax.nn.gelu, before_act)
    grad_before = gelu_back(grad_hidden)[0].astype(jnp.bfloat16)
    grad_feed_in = weight_grad(normed_ff, grad_before)
    grad_cross_res, grad_gain_ff = norm_back(
        after_cross, gain_ff, back_project(grad_before, feed_in)
    )
    grad_cross_res = cotangent.astype(jnp.float32) + grad_cross_res
    cross_branch = grad_cross_res.astype(jnp.bfloat16)
    grad_cross_output = weight_grad(cross_context, cross_branch)
    grad_cross_ctx = back_project(cross_branch, cross_output).astype(jnp.bfloat16)
    cross_delta = head_delta(grad_cross_ctx, cross_attn)
    all_keys, all_values, all_docs = (
        lax.all_gather(cross_keys, "blk", axis=1, tiled=True),
        lax.all_gather(cross_values, "blk", axis=1, tiled=True),
        lax.all_gather(key_docs, "blk", axis=1, tiled=True),
    )

    def passage_step(running, block_index):
        offset = block_index * enc_shard
        piece_keys = lax.dynamic_slice_in_dim(all_keys, offset, enc_shard, 1)
        piece_values = lax.dynamic_slice_in_dim(all_values, offset, enc_shard, 1)
        piece_docs = lax.dynamic_slice_in_dim(all_docs, offset, enc_shard, 1)
        allowed = dec_seg[:, :, None] == piece_docs[:, None, :]
        grad_query, grad_kv = grad_pair(
            cross_queries, grad_cross_ctx, cross_lse, cross_delta, piece_keys, piece_values, allowed
        )
        return (running + grad_query, grad_kv)

    grad_cross_q, key_terms = lax.scan(
        passage_step, jnp.zeros((row_count, tok_shard, width), jnp.float32), block_ids
    )
    grad_cross_kv = lax.psum_scatter(
        key_terms.astype(jnp.bfloat16), "blk", scatter_dimension=0, tiled=True
    ).astype(jnp.float32)[0]
    low_cross_q = grad_cross_q.astype(jnp.bfloat16)
    low_cross_k = grad_cross_kv[..., :width].astype(jnp.bfloat16)
    low_cross_v = grad_cross_kv[..., width:].astype(jnp.bfloat16)
    grad_cross_query = weight_grad(normed_cross, low_cross_q)
    grad_cross_key = weight_grad(encoded, low_cross_k)
    grad_cross_value = weight_grad(encoded, low_cross_v)
    encoded_grad = back_project(low_cross_k, cross_key) + back_project(low_cross_v, cross_value)
    grad_self_res, grad_gain_cross = norm_back(
        after_self, gain_cross, back_project(low_cross_q, cross_query)
    )
    grad_self_res = grad_cross_res + grad_self_res
    self_branch = grad_self_res.astype(jnp.bfloat16)
    grad_self_output = weight_grad(self_context, self_branch)
    grad_self_ctx = back_project(self_branch, self_output).astype(jnp.bfloat16)
    self_delta = head_delta(grad_self_ctx, self_attn)
    all_self_keys, all_self_values, all_self_segs = (
        lax.all_gather(self_keys, "blk", axis=1, tiled=True),
        lax.all_gather(self_values, "blk", axis=1, tiled=True),
        lax.all_gather(dec_seg, "blk", axis=1, tiled=True),
    )

    def self_step(running, block_index):
        offset = block_index * tok_shard
        piece_keys = lax.dynamic_slice_in_dim(all_self_keys, offset, tok_shard, 1)
        piece_values = lax.dynamic_slice_in_dim(all_self_values, offset, tok_shard, 1)
        piece_segs = lax.dynamic_slice_in_dim(all_self_segs, offset, tok_shard, 1)
        key_places = offset + jnp.arange(tok_shard)
        allowed = (dec_seg[:, :, None] == piece_segs[:, None, :]) & (
            key_places[None, None, :] <= query_places[None, :, None]
        )
        grad_query, grad_kv = grad_pair(
            self_queries, grad_self_ctx, self_lse, self_delta, piece_keys, piece_values, allowed
        )
        return (running + grad_query, grad_kv)

    grad_self_q, self_terms = lax.scan(
        self_step, jnp.zeros((row_count, tok_shard, width), jnp.float32), block_ids
    )
    grad_self_kv = lax.psum_scatter(
        self_terms.astype(jnp.bfloat16), "blk", scatter_dimension=0, tiled=True
    ).astype(jnp.float32)[0]
    low_self_q = grad_self_q.astype(jnp.bfloat16)
    low_self_k = grad_self_kv[..., :width].astype(jnp.bfloat16)
    low_self_v = grad_self_kv[..., width:].astype(jnp.bfloat16)
    grad_self_query = weight_grad(normed_self, low_self_q)
    grad_self_key = weight_grad(normed_self, low_self_k)
    grad_self_value = weight_grad(normed_self, low_self_v)
    grad_normed = (
        back_project(low_self_q, self_query)
        + back_project(low_self_k, self_key)
        + back_project(low_self_v, self_value)
    )
    grad_first, grad_gain_self = norm_back(residual, gain_self, grad_normed)
    input_grad = grad_self_res + grad_first
    matrices = (
        grad_self_query,
        grad_self_key,
        grad_self_value,
        grad_self_output,
        grad_cross_query,
        grad_cross_key,
        grad_cross_value,
        grad_cross_output,
        grad_feed_in,
        grad_feed_out,
    )
    spread_mats = tuple((spread_matrix(matrix, row_split, block_count) for matrix in matrices))
    spread_gains = tuple(
        (
            spread_gain(vector, row_split, block_count)
            for vector in (grad_gain_self, grad_gain_cross, grad_gain_ff)
        )
    )
    summed = (
        lax.psum_scatter(spread_mats[0], ("rows", "blk"), scatter_dimension=0, tiled=True),
        lax.psum_scatter(spread_mats[1], ("rows", "blk"), scatter_dimension=0, tiled=True),
        lax.psum_scatter(spread_mats[2], ("rows", "blk"), scatter_dimension=0, tiled=True),
        lax.psum_scatter(spread_mats[3], ("rows", "blk"), scatter_dimension=0, tiled=True),
        lax.psum_scatter(spread_mats[4], ("rows", "blk"), scatter_dimension=0, tiled=True),
        lax.psum_scatter(spread_mats[5], ("rows", "blk"), scatter_dimension=0, tiled=True),
        lax.psum_scatter(spread_mats[6], ("rows", "blk"), scatter_dimension=0, tiled=True),
        lax.psum_scatter(spread_mats[7], ("rows", "blk"), scatter_dimension=0, tiled=True),
        lax.psum_scatter(spread_mats[8], ("rows", "blk"), scatter_dimension=0, tiled=True),
        lax.psum_scatter(spread_mats[9], ("rows", "blk"), scatter_dimension=0, tiled=True),
        lax.psum_scatter(spread_gains[0], ("rows", "blk"), scatter_dimension=0, tiled=True),
        lax.psum_scatter(spread_gains[1], ("rows", "blk"), scatter_dimension=0, tiled=True),
        lax.psum_scatter(spread_gains[2], ("rows", "blk"), scatter_dimension=0, tiled=True),
    )
    return (
        output,
        input_grad,
        encoded_grad,
        summed[0][0],
        summed[1][0],
        summed[2][0],
        summed[3][0],
        summed[4][0],
        summed[5][0],
        summed[6][0],
        summed[7][0],
        summed[8][0],
        summed[9][0],
        summed[10][0],
        summed[11][0],
        summed[12][0],
    )


def solution(mesh):
    in_specs = (
        P("rows", "blk", None),
        P("rows", "blk", None),
        P("rows", "blk", None),
        P("rows", "blk"),
        P("rows", "blk"),
        P("rows", "blk"),
        P(),
        P(),
        P(),
        P(),
        P(),
        P(),
        P(),
        P(),
        P(),
        P(),
        P(),
        P(),
        P(),
    )
    out_specs = (
        P("rows", "blk", None),
        P("rows", "blk", None),
        P("rows", "blk", None),
        P("rows", "blk"),
        P("rows", "blk"),
        P("rows", "blk"),
        P("rows", "blk"),
        P("rows", "blk"),
        P("rows", "blk"),
        P("rows", "blk"),
        P("rows", "blk"),
        P("rows", "blk"),
        P("rows", "blk"),
        P("rows"),
        P("rows"),
        P("rows"),
    )
    return jax.shard_map(local, mesh=mesh, in_specs=in_specs, out_specs=out_specs, check_vma=False)
```

profile of v0, /device:TPU:0, one launch (start us, length us, event | category | flops | bytes accessed | tf_op | source)
XLA Modules:
  0.0 1700.4 jit_solution(5536791389779752275)
XLA Ops:
  50.9 12.2 all-gather.15.cloned.1.call-done
  67.4 24.2 %all-gather.9.cloned.1.call-done = bf16[1792,768]{1,0:T(8,128)(2,1)} async-done(((bf16[448,768]{1,0:T(8,128)(2,1)}), bf16[1792,768]{1,0:T(8,128)(2,1)}) %all-gather.9.cloned.1.call-update) | async-done | bytes 2752528 | tf_op jit(solution)/shard_map/all_gather | solution.py:176
  96.1 17.8 %select_reduce_fusion = (f32[12,448]{1,0:T(8,128)S(1)}, f32[12,448,1792]{2,1,0:T(8,128)}) fusion(pred[448,1792]{1,0:T(8,128)(4,1)} %fusion.46, bf16[448,12,64]{0,2,1:T(8,128)(2,1)} %bitcast.619, bf16[1792,12,64]{0,2,1:T(8,128)(2,1)} %bitcast.593), kind=kOutput, calls=%fused_computation.38 | convolution fusion | flops 1262021376 | bytes 42800128 | tf_op jit(solution)/shard_map/rqhe,rkhe->rhqk/dot_general | solution.py:48
  113.9 17.8 %fusion.18 = f32[12,448]{1,0:T(8,128)S(1)} fusion(f32[12,448,1792]{2,1,0:T(8,128)} %get-tuple-element.389, f32[12,448]{1,0:T(8,128)S(1)} %broadcast_maximum_fusion.1, pred[448,1792]{1,0:T(8,128)(4,1)S(1)} %copy-done.7), kind=kLoop, calls=%fused_computation.41 | loop fusion | flops 38529792 | bytes 39380992 | tf_op jit(solution)/shard_map/reduce_sum | solution.py:72
  137.6 17.6 %fusion.91 = (bf16[12,448,64]{1,2,0:T(8,128)(2,1)S(1)}, f32[12,448,64]{1,2,0:T(8,128)}) fusion(f32[12,448]{1,0:T(8,128)} %copy-done.52, bf16[1792,12,64]{0,2,1:T(8,128)(2,1)} %bitcast.636, f32[12,448,1792]{2,1,0:T(8,128)} %get-tuple-element.389, f32[12,448]{1,0:T(8,128)} %copy-done.54, pred[448,1792]{1,0:T(8,128)(4,1)} %fusion.46), kind=kOutput, calls=%fused_computation.155 | convolution fusion | flops 1272348672 | bytes 44197888 | tf_op jit(solution)/shard_map/rhqk,rkhe->rhqe/dot_general | solution.py:73
  161.2 15.3 select_reduce_fusion.1
  176.5 15.9 fusion.20
  193.1 15.9 fusion.133
  211.2 11.5 fusion.42
  222.7 9.7 fusion.52
  243.6 109.5 %while.26 = (s32[]{:T(128)}, f32[1,448,768]{1,2,0:T(8,128)}, bf16[4,1,384,1536]{2,3,1,0:T(8,128)(2,1)}, s32[4]{0:T(128)S(1)}, bf16[1,1536,768]{2,1,0:T(8,128)(2,...) while((s32[]{:T(128)}, f32[1,448,768]{1,2,0:T(8,128)}, ...), condition=%wide.region_9.10_spmd.clone, body=%wide.region_8.9_spmd.clone.sunk | while | flops 1346002944 | bytes 96200416 | solution.py:236
  365.3 133.3 %while.27 = (s32[]{:T(128)}, f32[1,448,768]{1,2,0:T(8,128)}, bf16[4,1,448,1536]{2,3,1,0:T(8,128)(2,1)}, s32[4]{0:T(128)S(1)}, bf16[1,1792,768]{2,1,0:T(8,128)(2,...) while((s32[]{:T(128)}, f32[1,448,768]{1,2,0:T(8,128)}, ...), condition=%wide.region_12.13_spmd.clone, body=%wide.region_11.12_spmd.clone.sunk | while | flops 1570567040 | bytes 99968336 | solution.py:277
  547.9 9.7 reduce-scatter.13.cloned.1.call-done
  585.6 40.7 %all-reduce.4 = (f32[32,96]{1,0:T(8,128)S(1)}, f32[32,96]{1,0:T(8,128)S(1)}, f32[32,96]{1,0:T(8,128)S(1)}) all-reduce(f32[32,96]{1,0:T(8,128)S(1)} %bitcast.659, f32[32,96]{1,0:T(8,128)S(1)} %bitcast.660, f32[32,96]{1,0:T(8,128)S(1)} %bitcast.661), channel_id=18, replica_groups=mesh['rows'=8,'blk'=4] {'rows','blk'}, use_global_device_ids=true, to_apply=%region_27.28.clone | all-reduce | flops 9216 | bytes 73728
  630.1 35.1 %reduce-scatter.23.cloned.1.call-done = f32[1,96,192]{2,1,0:T(8,128)} async-done(((f32[32,96,192]{2,1,0:T(8,128)}), f32[1,96,192]{2,1,0:T(8,128)}) %reduce-scatter.23.cloned.1.call-update) | async-done | bytes 73744 | tf_op jit(solution)/shard_map/reduce_scatter | solution.py:319
  665.2 106.5 %reduce-scatter.25.cloned.1.call-done = f32[1,96,192]{2,1,0:T(8,128)} async-done(((f32[32,96,192]{2,1,0:T(8,128)}), f32[1,96,192]{2,1,0:T(8,128)}) %reduce-scatter.25.cloned.1.call-update) | async-done | bytes 73744 | tf_op jit(solution)/shard_map/reduce_scatter | solution.py:320
  771.7 106.5 %reduce-scatter.31.cloned.1.call-done = f32[1,96,192]{2,1,0:T(8,128)} async-done(((f32[32,96,192]{2,1,0:T(8,128)}), f32[1,96,192]{2,1,0:T(8,128)}) %reduce-scatter.31.cloned.1.call-update) | async-done | bytes 73744 | tf_op jit(solution)/shard_map/reduce_scatter | solution.py:323
  878.2 106.4 %reduce-scatter.27.cloned.1.call-done = f32[1,96,192]{2,1,0:T(8,128)} async-done(((f32[32,96,192]{2,1,0:T(8,128)}), f32[1,96,192]{2,1,0:T(8,128)}) %reduce-scatter.27.cloned.1.call-update) | async-done | bytes 73744 | tf_op jit(solution)/shard_map/reduce_scatter | solution.py:321
  984.6 106.5 %reduce-scatter.29.cloned.1.call-done = f32[1,96,192]{2,1,0:T(8,128)} async-done(((f32[32,96,192]{2,1,0:T(8,128)}), f32[1,96,192]{2,1,0:T(8,128)}) %reduce-scatter.29.cloned.1.call-update) | async-done | bytes 73744 | tf_op jit(solution)/shard_map/reduce_scatter | solution.py:322
  1091.1 140.8 %reduce-scatter.33.cloned.1.call-done = f32[1,96,768]{2,1,0:T(8,128)} async-done(((f32[32,96,768]{2,1,0:T(8,128)}), f32[1,96,768]{2,1,0:T(8,128)}) %reduce-scatter.33.cloned.1.call-update) | async-done | bytes 294928 | tf_op jit(solution)/shard_map/reduce_scatter | solution.py:324
  1232.0 142.1 %reduce-scatter.35.cloned.1.call-done = f32[1,384,192]{1,2,0:T(8,128)} async-done(((f32[32,384,192]{1,2,0:T(8,128)}), f32[1,384,192]{1,2,0:T(8,128)}) %reduce-scatter.35.cloned.1.call-update) | async-done | bytes 294928 | tf_op jit(solution)/shard_map/reduce_scatter | solution.py:325
  1374.0 106.6 %reduce-scatter.17.cloned.1.call-done = f32[1,96,192]{2,1,0:T(8,128)} async-done(((f32[32,96,192]{2,1,0:T(8,128)}), f32[1,96,192]{2,1,0:T(8,128)}) %reduce-scatter.17.cloned.1.call-update) | async-done | bytes 73744 | tf_op jit(solution)/shard_map/reduce_scatter | solution.py:316
  1480.6 106.4 %reduce-scatter.19.cloned.1.call-done = f32[1,96,192]{2,1,0:T(8,128)} async-done(((f32[32,96,192]{2,1,0:T(8,128)}), f32[1,96,192]{2,1,0:T(8,128)}) %reduce-scatter.19.cloned.1.call-update) | async-done | bytes 73744 | tf_op jit(solution)/shard_map/reduce_scatter | solution.py:317
  1587.0 106.4 %reduce-scatter.21.cloned.1.call-done = f32[1,96,192]{2,1,0:T(8,128)} async-done(((f32[32,96,192]{2,1,0:T(8,128)}), f32[1,96,192]{2,1,0:T(8,128)}) %reduce-scatter.21.cloned.1.call-update) | async-done | bytes 73744 | tf_op jit(solution)/shard_map/reduce_scatter | solution.py:318
  (486 shorter events, 405.7 us)
Async XLA Ops:
  7.2 201.8 %copy-start = (bf16[768,768]{1,0:T(8,128)(2,1)S(1)}, bf16[768,768]{1,0:T(8,128)(2,1)}, u32[]{:S(2)}) copy-start(bf16[768,768]{1,0:T(8,128)(2,1)} %param.36) | copy-start | bytes 3538948
  7.2 40.4 %all-gather.13.cloned.1.call-start = ((), (), s32[]{:S(2)}) async-start(), calls=%async_computation.26 | async-start | bytes 2949120 | tf_op jit(solution)/shard_map/all_gather | solution.py:193
  10.3 52.8 %all-gather.15.cloned.1.call-start = ((), (), s32[]{:S(2)}) async-start(), calls=%async_computation.27 | async-start | bytes 2949120 | tf_op jit(solution)/shard_map/all_gather | solution.py:194
  13.4 78.2 %all-gather.9.cloned.1.call-start = ((), (), s32[]{:S(2)}) async-start(), calls=%async_computation.24 | async-start | bytes 3440640 | tf_op jit(solution)/shard_map/all_gather | solution.py:176
  15.3 117.7 %all-gather.11.cloned.1.call-start = ((), (), s32[]{:S(2)}) async-start(), calls=%async_computation.25 | async-start | bytes 3440640 | tf_op jit(solution)/shard_map/all_gather | solution.py:177
  18.3 494.4 %reduce-scatter.15.cloned.1.call-start = ((), (), s32[]{:S(2)}) async-start(), calls=%async_computation.13 | async-start | bytes 5898240 | tf_op jit(solution)/shard_map/reduce_scatter | solution.py:239
  96.1 17.8 %copy-start.7 = (pred[448,1792]{1,0:T(8,128)(4,1)S(1)}, pred[448,1792]{1,0:T(8,128)(4,1)}, u32[]{:S(2)}) copy-start(pred[448,1792]{1,0:T(8,128)(4,1)} %fusion.46) | copy-start | bytes 2408452
  113.9 17.9 %copy-start.54 = (f32[12,448]{1,0:T(8,128)}, f32[12,448]{1,0:T(8,128)S(1)}, u32[]{:S(2)}) copy-start(f32[12,448]{1,0:T(8,128)S(1)} %broadcast_maximum_fusion.1) | copy-start | bytes 64516
  211.2 23.2 %copy-start.8 = (f32[1,448,768]{2,1,0:T(8,128)}, f32[1,448,768]{2,1,0:T(8,128)S(1)}, u32[]{:S(2)}) copy-start(f32[1,448,768]{2,1,0:T(8,128)S(1)} %get-tuple-element.399) | copy-start | bytes 4128772
  363.6 194.0 %reduce-scatter.13.cloned.1.call-start = ((), (), s32[]{:S(2)}) async-start(), calls=%async_computation.12 | async-start | bytes 7864320 | tf_op jit(solution)/shard_map/reduce_scatter | solution.py:280
  498.7 166.5 %reduce-scatter.23.cloned.1.call-start = ((), (), s32[]{:S(2)}) async-start(), calls=%async_computation.17 | async-start | bytes 3244032 | tf_op jit(solution)/shard_map/reduce_scatter | solution.py:319
  502.8 268.9 %reduce-scatter.25.cloned.1.call-start = ((), (), s32[]{:S(2)}) async-start(), calls=%async_computation.18 | async-start | bytes 3244032 | tf_op jit(solution)/shard_map/reduce_scatter | solution.py:320
  506.9 371.3 %reduce-scatter.31.cloned.1.call-start = ((), (), s32[]{:S(2)}) async-start(), calls=%async_computation.21 | async-start | bytes 3244032 | tf_op jit(solution)/shard_map/reduce_scatter | solution.py:323
  511.3 473.3 %reduce-scatter.27.cloned.1.call-start = ((), (), s32[]{:S(2)}) async-start(), calls=%async_computation.19 | async-start | bytes 3244032 | tf_op jit(solution)/shard_map/reduce_scatter | solution.py:321
  520.7 570.4 %reduce-scatter.29.cloned.1.call-start = ((), (), s32[]{:S(2)}) async-start(), calls=%async_computation.20 | async-start | bytes 3244032 | tf_op jit(solution)/shard_map/reduce_scatter | solution.py:322
  527.2 704.8 %reduce-scatter.33.cloned.1.call-start = ((), (), s32[]{:S(2)}) async-start(), calls=%async_computation.22 | async-start | bytes 9732096 | tf_op jit(solution)/shard_map/reduce_scatter | solution.py:324
  535.4 838.6 %reduce-scatter.35.cloned.1.call-start = ((), (), s32[]{:S(2)}) async-start(), calls=%async_computation.23 | async-start | bytes 9732096 | tf_op jit(solution)/shard_map/reduce_scatter | solution.py:325
  544.3 936.3 %reduce-scatter.17.cloned.1.call-start = ((), (), s32[]{:S(2)}) async-start(), calls=%async_computation.14 | async-start | bytes 3244032 | tf_op jit(solution)/shard_map/reduce_scatter | solution.py:316
  567.1 1019.9 %reduce-scatter.19.cloned.1.call-start = ((), (), s32[]{:S(2)}) async-start(), calls=%async_computation.15 | async-start | bytes 3244032 | tf_op jit(solution)/shard_map/reduce_scatter | solution.py:317
  570.0 1123.4 %reduce-scatter.21.cloned.1.call-start = ((), (), s32[]{:S(2)}) async-start(), calls=%async_computation.16 | async-start | bytes 3244032 | tf_op jit(solution)/shard_map/reduce_scatter | solution.py:318
  583.7 43.6 %copy-start.66 = (f32[448]{0:T(512)S(1)}, f32[448]{0:T(512)}, u32[]{:S(2)}) copy-start(f32[448]{0:T(512)} %copy-done.65) | copy-start | bytes 5380
  583.7 43.6 %copy-start.14 = (f32[448,768]{1,0:T(8,128)S(1)}, f32[448,768]{1,0:T(8,128)}, u32[]{:S(2)}) copy-start(f32[448,768]{1,0:T(8,128)} %copy-done.13) | copy-start | bytes 4128772
  583.7 43.6 %copy-start.23 = (bf16[1,448,768]{2,1,0:T(8,128)(2,1)S(1)}, bf16[1,448,768]{2,1,0:T(8,128)(2,1)}, u32[]{:S(2)}) copy-start(bf16[1,448,768]{2,1,0:T(8,128)(2,1)} %param.23) | copy-start | bytes 2064388
  583.7 1109.7 %copy-start.1 = (bf16[768,768]{1,0:T(8,128)(2,1)S(1)}, bf16[768,768]{1,0:T(8,128)(2,1)}, u32[]{:S(2)}) copy-start(bf16[768,768]{1,0:T(8,128)(2,1)} %param.36) | copy-start | bytes 3538948
  (112 other events, 496.6 us)
Sparse Core Ops, SparseCore 0:
  10.4 27.0 all-gather.12
  39.0 23.9 all-gather.14
  65.2 26.2 all-gather.8
  93.0 26.3 all-gather.10
  363.8 48.0 reduce-scatter.14
  498.8 58.6 reduce-scatter.12
  563.6 101.5 reduce-scatter.22
  671.2 100.4 reduce-scatter.24
  777.7 100.4 reduce-scatter.30
  884.1 100.4 reduce-scatter.26
  990.6 100.4 reduce-scatter.28
  1097.5 134.4 reduce-scatter.32
  1239.5 134.5 reduce-scatter.34
  1379.9 100.6 reduce-scatter.16
  1486.4 100.5 reduce-scatter.18
  1592.9 100.4 reduce-scatter.20
where the time goes:
time: 1710 us; the launch traced here: 1700 us
  waiting for transfers between devices  1110 us (65%)
  matrix products  335 us (20%)
  local copies, waits for them, and re-layouts  93.1 us (5%)
  other arithmetic  85.9 us (5%)
  blocking collectives  52.4 us (3%)
    reduce_scatter x1, waiting for transfers between devices, local(): lax.psum_scatter(spread_mats[9], ('rows', 'blk'), scatter_dimension=0, ti...  142 us
    reduce_scatter x1, waiting for transfers between devices, local(): lax.psum_scatter(spread_mats[8], ('rows', 'blk'), scatter_dimension=0, ti...  141 us
    reduce_scatter x1, waiting for transfers between devices, local(): lax.psum_scatter(spread_mats[0], ('rows', 'blk'), scatter_dimension=0, ti...  107 us
    reduce_scatter x1, waiting for transfers between devices, local(): lax.psum_scatter(spread_mats[6], ('rows', 'blk'), scatter_dimension=0, ti...  107 us
    reduce_scatter x1, waiting for transfers between devices, local(): lax.psum_scatter(spread_mats[7], ('rows', 'blk'), scatter_dimension=0, ti...  107 us
    reduce_scatter x1, waiting for transfers between devices, local(): lax.psum_scatter(spread_mats[4], ('rows', 'blk'), scatter_dimension=0, ti...  107 us
    reduce_scatter x1, waiting for transfers between devices, local(): lax.psum_scatter(spread_mats[1], ('rows', 'blk'), scatter_dimension=0, ti...  106 us
    reduce_scatter x1, waiting for transfers between devices, local(): lax.psum_scatter(spread_mats[2], ('rows', 'blk'), scatter_dimension=0, ti...  106 us
  transfers between devices with their start and end apart: 16, of which 13 were waited for; matrix products, arithmetic and copies ran while one was open for 16% of the time, Pallas kernels for 0%

commit v1 on v0

--- a/solution.py
+++ b/solution.py
@@ -1,6 +1,8 @@
 import jax
 import jax.numpy as jnp
 from jax import lax
+from jax.experimental import pallas as pl
+from jax.experimental.pallas import tpu as pltpu
 from jax.sharding import PartitionSpec as P
 
 HEADS = 12
@@ -140,7 +142,7 @@
     )
 
 
-def local(
+def local_any(
     inputs,
     encoded,
     cotangent,
@@ -347,7 +349,940 @@
     )
 
 
+BF16 = jnp.bfloat16
+F32 = jnp.float32
+LANES = 128
+HALF = 2 * LANES + LANES
+CORE_SWAP = ((0, 1), (1, 0), (2, 3), (3, 2))
+CHIP_SWAP = ((0, 2), (2, 0), (1, 3), (3, 1))
+
+
+def dot_nn(left, right):
+    return jnp.dot(left, right, preferred_element_type=F32)
+
+
+def dot_nt(left, right):
+    return lax.dot_general(left, right, (((1,), (1,)), ((), ())), preferred_element_type=F32)
+
+
+def dot_tn(left, right):
+    return lax.dot_general(left, right, (((0,), (0,)), ((), ())), preferred_element_type=F32)
+
+
+def whole(array):
+    rank = len(array.shape)
+    return pl.BlockSpec(array.shape, lambda *_: (0,) * rank)
+
+
+def struct(shape, dtype):
+    return jax.ShapeDtypeStruct(shape, dtype)
+
+
+def run_kernel(name, body, scalars, args, in_specs, outs, out_specs, grid=(1,), scratch=(), flops=0):
+    moved = sum(a.size * a.dtype.itemsize for a in args)
+    moved += sum(o.size * o.dtype.itemsize for o in outs)
+    return pl.pallas_call(
+        body,
+        grid_spec=pltpu.PrefetchScalarGridSpec(
+            num_scalar_prefetch=1,
+            grid=grid,
+            in_specs=list(in_specs),
+            out_specs=list(out_specs),
+            scratch_shapes=list(scratch),
+        ),
+        out_shape=list(outs),
+        compiler_params=pltpu.CompilerParams(vmem_limit_bytes=58 << 20),
+        cost_estimate=pl.CostEstimate(flops=int(flops), bytes_accessed=int(moved), transcendentals=0),
+        name=name,
+    )(scalars, *args)
+
+
+def unit_norm(values):
+    scale = lax.rsqrt(jnp.mean(values * values, axis=-1, keepdims=True) + 1e-06)
+    return (values * scale, scale)
+
+
+def norm_pull(values, gain_vec, grad_out):
+    normal, scale = unit_norm(values)
+    scaled = grad_out * gain_vec
+    inner = jnp.mean(scaled * normal, axis=-1, keepdims=True)
+    return (scale * (scaled - normal * inner), jnp.sum(grad_out * normal, axis=0, keepdims=True))
+
+
+def projections(name, place, mine, other, gain_vec, weights, scales):
+    tok, width = mine.shape
+    count = len(weights)
+
+    def body(s, mine_ref, other_ref, gain_ref, *refs):
+        weight_refs, normed_ref, out_refs = refs[:count], refs[count], refs[count + 1 :]
+        for source, part in ((mine_ref, s[0]), (other_ref, 1 - s[0])):
+            rows = pl.ds(pl.multiple_of(part * tok, tok), tok)
+            normed = (unit_norm(source[...].astype(F32))[0] * gain_ref[...]).astype(BF16)
+            normed_ref[rows, :] = normed
+            for weight_ref, out_ref, scale in zip(weight_refs, out_refs, scales):
+                out_ref[rows, :] = (dot_nn(normed, weight_ref[...]) * scale).astype(BF16)
+
+    columns = pl.BlockSpec((width, HALF), lambda _, s: (0, s[0]))
+    outs = [struct((2 * tok, width), BF16)] + [struct((2 * tok, HALF), BF16)] * count
+    return run_kernel(
+        name,
+        body,
+        place,
+        (mine, other, gain_vec, *weights),
+        [whole(mine), whole(other), whole(gain_vec)] + [columns] * count,
+        outs,
+        [whole(o) for o in outs],
+        flops=4 * tok * width * HALF * count,
+    )
+
+
+def passage_pair(place, first, second, key_weight, value_weight):
+    enc, width = first.shape
+
+    def body(s, first_ref, second_ref, key_w_ref, value_w_ref, key_ref, value_ref):
+        for at, source in enumerate((first_ref, second_ref)):
+            rows = pl.ds(at * enc, enc)
+            key_ref[rows, :] = dot_nn(source[...], key_w_ref[...]).astype(BF16)
+            value_ref[rows, :] = dot_nn(source[...], value_w_ref[...]).astype(BF16)
+
+    args = (first, second, key_weight, value_weight)
+    outs = [struct((2 * enc, width), BF16)] * 2
+    return run_kernel(
+        "passage_pair",
+        body,
+        place,
+        args,
+        [whole(a) for a in args],
+        outs,
+        [whole(o) for o in outs],
+        flops=8 * enc * width * width,
+    )
+
+
+def head_lanes():
+    lane = lax.broadcasted_iota(jnp.int32, (1, LANES), 1)
+    return (lane, (lane < HEAD_DIM, lane >= HEAD_DIM))
+
+
+def only(keep, values):
+    return jnp.where(keep, values, jnp.zeros_like(values))
+
+
+def soft_block(queries, marks, keys, values, causal):
+    lane, masks = head_lanes()
+    rows, cols = queries.shape[0], keys.shape[0]
+    attended, sums = ([], [])
+    for keep in masks:
+        scores = dot_nt(jnp.concatenate([only(keep, queries), marks], axis=1), keys)
+        if causal:
+            at_row = lax.broadcasted_iota(jnp.int32, (rows, rows), 0)
+            at_col = lax.broadcasted_iota(jnp.int32, (rows, rows), 1)
+            last = jnp.where(at_col <= at_row, scores[:, cols - rows :], NEG_FILL)
+            scores = last if cols == rows else jnp.concatenate([scores[:, : cols - rows], last], axis=1)
+        top = jnp.max(scores, axis=1, keepdims=True)
+        weights = jnp.exp(scores - top)
+        total = jnp.sum(weights, axis=1, keepdims=True)
+        attended.append(dot_nn(weights.astype(BF16), values) / total)
+        sums.append(top + jnp.log(total))
+    return (jnp.where(masks[0], *attended), jnp.where(masks[0], *sums))
+
+
+def three_parts(lane, column, base):
+    high = column.astype(BF16)
+    rest = column - high.astype(F32)
+    middle = rest.astype(BF16)
+    low = (rest - middle.astype(F32)).astype(BF16)
+    out = jnp.where(lane == 3, -high, base)
+    out = jnp.where(lane == 4, -middle, out)
+    return jnp.where(lane == 5, -low, out)
+
+
+def pull_block(queries, marks, keys, key_marks, values, grads, attended, sums, causal):
+    lane, masks = head_lanes()
+    rows, cols = queries.shape[0], keys.shape[0]
+    wide_keys = jnp.concatenate([keys, key_marks], axis=1)
+    ones = jnp.where((lane >= 3) & (lane < 6), 1.0, 0.0).astype(BF16)
+    wide_values = jnp.concatenate([values, jnp.broadcast_to(ones, (cols, LANES))], axis=1)
+    product = grads.astype(F32) * attended
+    flipped = keys.T
+    grad_queries = []
+    grad_keys = grad_values = None
+    for at, keep in enumerate(masks):
+        query, grad = (only(keep, queries), only(keep, grads))
+        delta = jnp.sum(jnp.where(keep, product, 0.0), axis=1, keepdims=True)
+        log_sum = sums[:, HEAD_DIM * at : HEAD_DIM * at + 1]
+        wide_query = jnp.concatenate([query, three_parts(lane, log_sum, marks)], axis=1)
+        wide_grad = jnp.concatenate([grad, three_parts(lane, delta, jnp.zeros_like(marks))], axis=1)
+        probs = jnp.exp(dot_nt(wide_keys, wide_query))
+        if causal:
+            at_row = lax.broadcasted_iota(jnp.int32, (rows, rows), 0)
+            at_col = lax.broadcasted_iota(jnp.int32, (rows, rows), 1)
+            last = jnp.where(at_row <= at_col, probs[cols - rows :, :], 0.0)
+            probs = last if cols == rows else jnp.concatenate([probs[: cols - rows, :], last], axis=0)
+        grad_scores = (probs * dot_nt(wide_values, wide_grad)).astype(BF16)
+        grad_queries.append(dot_nn(flipped, grad_scores))
+        key_part = dot_nn(grad_scores, query)
+        value_part = dot_nn(probs.astype(BF16), grad)
+        grad_keys = key_part if at == 0 else grad_keys + key_part
+        grad_values = value_part if at == 0 else grad_values + value_part
+    sub = lax.broadcasted_iota(jnp.int32, (LANES, 1), 0)
+    return (jnp.where(sub < HEAD_DIM, *grad_queries).T * SCALE, grad_keys, grad_values)
+
+
+def pair_columns(array):
+    return pl.BlockSpec((array.shape[0], LANES), lambda p, _: (0, p))
+
+
+def near_attention(place, queries, keys, values, marks, key_marks):
+    both, width = queries.shape
+    tok = both // 2
+
+    def body(s, q_ref, k_ref, v_ref, m_ref, km_ref, out_ref, sum_ref):
+        for at in (0, 1):
+            rows, seen = (pl.ds(at * tok, tok), pl.ds(0, (at + 1) * tok))
+            wide = jnp.concatenate([k_ref[seen, :], km_ref[seen, :]], axis=1)
+            out_ref[rows, :], sum_ref[rows, :] = soft_block(q_ref[rows, :], m_ref[rows, :], wide, v_ref[seen, :], True)
+
+    args = (queries, keys, values, marks, key_marks)
+    outs = [struct((both, width), F32)] * 2
+    return run_kernel(
+        "near_attention",
+        body,
+        place,
+        args,
+        [pair_columns(a) for a in args[:3]] + [whole(a) for a in args[3:]],
+        outs,
+        [pair_columns(o) for o in outs],
+        grid=(width // LANES,),
+        flops=both * both * 0.75 * 8 * 2 * width,
+    )
+
+
+def far_attention(place, queries, keys, values, marks, key_marks, near_out, near_sum):
+    both, width = queries.shape
+    tok = both // 2
+
+    def body(s, q_ref, k_ref, v_ref, m_ref, km_ref, no_ref, ns_ref, out_ref, sum_ref, keep_ref, send_ref):
+        def write(at, out, log_sum):
+            rows = pl.ds(at * tok, tok)
+            out_ref[rows, :] = out
+            sum_ref[rows, :] = log_sum
+
+            @pl.when(s[0] == at)
+            def _():
+                keep_ref[...] = out.astype(BF16)
+
+            @pl.when(s[0] != at)
+            def _():
+                send_ref[...] = out.astype(BF16)
+
+        @pl.when(s[1] == 0)
+        def _():
+            for at in (0, 1):
+                rows = pl.ds(at * tok, tok)
+                write(at, no_ref[rows, :], ns_ref[rows, :])
+
+        @pl.when(s[1] != 0)
+        def _():
+            wide = jnp.concatenate([k_ref[...], km_ref[...]], axis=1)
+            for at in (0, 1):
+                rows = pl.ds(at * tok, tok)
+                out, log_sum = soft_block(q_ref[rows, :], m_ref[rows, :], wide, v_ref[...], False)
+                near_log = ns_ref[rows, :]
+                top = jnp.maximum(near_log, log_sum)
+                near_part, far_part = (jnp.exp(near_log - top), jnp.exp(log_sum - top))
+                total = near_part + far_part
+                write(at, (no_ref[rows, :] * near_part + out * far_part) / total, top + jnp.log(total))
+
+    args = (queries, keys, values, marks, key_marks, near_out, near_sum)
+    outs = [struct((both, width), F32)] * 2 + [struct((tok, width), BF16)] * 2
+    columns = [pair_columns(a) for a in args]
+    columns[3], columns[4] = whole(marks), whole(key_marks)
+    return run_kernel(
+        "far_attention",
+        body,
+        place,
+        args,
+        columns,
+        outs,
+        [pair_columns(o) for o in outs],
+        grid=(width // LANES,),
+        flops=both * both * 8 * 2 * width,
+    )
+
+
+def self_pull(name, place, near, queries, keys, values, marks, key_marks, grad_keep, grad_recv, attended, sums, carried):
+    both, width = queries.shape
+    tok = both // 2
+
+    def body(s, q_ref, k_ref, v_ref, m_ref, km_ref, gk_ref, gr_ref, at_ref, ls_ref, ca_ref, dq_ref, dk_ref, dv_ref, sum_k, sum_v):
+        def work():
+            for at in (0, 1):
+                rows = pl.ds(at * tok, tok)
+                count = (at + 1) * tok if near else both
+                seen = pl.ds(0, count)
+                grads = jnp.where(s[0] == at, gk_ref[...], gr_ref[...])
+                grad_q, grad_k, grad_v = pull_block(
+                    q_ref[rows, :], m_ref[rows, :], k_ref[seen, :], km_ref[seen, :], v_ref[seen, :], grads,
+                    at_ref[rows, :], ls_ref[rows, :], near,
+                )
+                if near:
+                    dq_ref[rows, :] = (grad_q + ca_ref[rows, :]).astype(BF16)
+                else:
+                    dq_ref[rows, :] = grad_q
+                if at == 0:
+                    sum_k[seen, :] = grad_k
+                    sum_v[seen, :] = grad_v
+                    if count < both:
+                        sum_k[pl.ds(count, both - count), :] = jnp.zeros((both - count, LANES), F32)
+                        sum_v[pl.ds(count, both - count), :] = jnp.zeros((both - count, LANES), F32)
+                else:
+                    dk_ref[...] = (sum_k[...] + grad_k).astype(BF16)
+                    dv_ref[...] = (sum_v[...] + grad_v).astype(BF16)
+
+        if near:
+            work()
+        else:
+            pl.when(s[1] != 0)(work)
+
+            @pl.when(s[1] == 0)
+            def _():
+                for ref in (dq_ref, dk_ref, dv_ref):
+                    ref[...] = jnp.zeros_like(ref)
+
+    args = (queries, keys, values, marks, key_marks, grad_keep, grad_recv, attended, sums, carried)
+    specs = [pair_columns(a) for a in args]
+    specs[3], specs[4] = whole(marks), whole(key_marks)
+    if not near:
+        specs[9] = whole(carried)
+    outs = [struct((both, width), BF16 if near else F32)] + [struct((both, width), BF16)] * 2
+    return run_kernel(
+        name,
+        body,
+        place,
+        args,
+        specs,
+        outs,
+        [pair_columns(o) for o in outs],
+        grid=(width // LANES,),
+        scratch=[pltpu.VMEM((both, LANES), F32)] * 2,
+        flops=both * both * (0.75 if near else 1.0) * 20 * 2 * width,
+    )
+
+
+def gather_slots(s, enc, target, first_ref, second_ref):
+    for at in range(4):
+        slot = s[at]
+        rows = pl.ds(at * enc, enc)
+
+        @pl.when(slot < 2)
+        def _():
+            target[rows, :] = first_ref[pl.ds(pl.multiple_of(slot * enc, enc), enc), :]
+
+        @pl.when(slot >= 2)
+        def _():
+            target[rows, :] = second_ref[pl.ds(pl.multiple_of((slot - 2) * enc, enc), enc), :]
+
+
+def by_count(s, work):
+    pl.when(s[4] <= 2)(lambda: work(2))
+    pl.when(s[4] == 3)(lambda: work(3))
+    pl.when(s[4] >= 4)(lambda: work(4))
+
+
+def cross_attention(needed, queries, keys, values, marks, key_marks):
+    tok, width = queries.shape
+    enc = keys[0].shape[0] // 2
+
+    def body(s, q_ref, k0_ref, k1_ref, v0_ref, v1_ref, m_ref, km0_ref, km1_ref, ctx_ref, out_ref, sum_ref, all_k, all_v):
+        keep = pl.ds(0, LANES)
+        gather_slots(s, enc, all_k.at[:, keep], k0_ref, k1_ref)
+        gather_slots(s, enc, all_v, v0_ref, v1_ref)
+
+        @pl.when(pl.program_id(0) == 0)
+        def _():
+            gather_slots(s, enc, all_k.at[:, pl.ds(LANES, LANES)], km0_ref, km1_ref)
+
+        def work(count):
+            seen = pl.ds(0, count * enc)
+            out, log_sum = soft_block(q_ref[...], m_ref[...], all_k[seen, :], all_v[seen, :], False)
+            ctx_ref[...] = out.astype(BF16)
+            out_ref[...] = out
+            sum_ref[...] = log_sum
+
+        by_count(s, work)
+
+    args = (queries, *keys, *values, marks, *key_marks)
+    outs = [struct((tok, width), BF16)] + [struct((tok, width), F32)] * 2
+    return run_kernel(
+        "cross_attention",
+        body,
+        needed,
+        args,
+        [pair_columns(a) for a in args[:5]] + [whole(a) for a in args[5:]],
+        outs,
+        [pair_columns(o) for o in outs],
+        grid=(width // LANES,),
+        scratch=[pltpu.VMEM((4 * enc, 2 * LANES), BF16), pltpu.VMEM((4 * enc, LANES), BF16)],
+        flops=tok * 2.5 * enc * 8 * 2 * width,
+    )
+
+
+def cross_pull(needed, queries, keys, values, marks, key_marks, grads, attended, sums):
+    tok, width = queries.shape
+    enc = keys[0].shape[0] // 2
+
+    def body(s, q_ref, k0_ref, k1_ref, v0_ref, v1_ref, m_ref, km0_ref, km1_ref, g_ref, at_ref, ls_ref, dq_ref, dk_ref, dv_ref, all_k, all_v, all_m):
+        gather_slots(s, enc, all_k, k0_ref, k1_ref)
+        gather_slots(s, enc, all_v, v0_ref, v1_ref)
+
+        @pl.when(pl.program_id(0) == 0)
+        def _():
+            gather_slots(s, enc, all_m, km0_ref, km1_ref)
+
+        def work(count):
+            seen = pl.ds(0, count * enc)
+            grad_q, grad_k, grad_v = pull_block(
+                q_ref[...], m_ref[...], all_k[seen, :], all_m[seen, :], all_v[seen, :], g_ref[...], at_ref[...],
+                ls_ref[...], False,
+            )
+            dq_ref[...] = grad_q.astype(BF16)
+            low_k, low_v = (grad_k.astype(BF16), grad_v.astype(BF16))
+            for at in range(4):
+                rows = pl.ds(pl.multiple_of(s[at] * enc, enc), enc)
+                if at < count:
+                    dk_ref[rows, :] = low_k[at * enc : (at + 1) * enc, :]
+                    dv_ref[rows, :] = low_v[at * enc : (at + 1) * enc, :]
+                else:
+                    dk_ref[rows, :] = jnp.zeros((enc, LANES), BF16)
+                    dv_ref[rows, :] = jnp.zeros((enc, LANES), BF16)
+
+        by_count(s, work)
+
+    args = (queries, *keys, *values, marks, *key_marks, grads, attended, sums)
+    specs = [pair_columns(a) for a in args]
+    for at in (5, 6, 7):
+        specs[at] = whole(args[at])
+    outs = [struct((tok, width), BF16)] + [struct((4 * enc, width), BF16)] * 2
+    return run_kernel(
+        "cross_pull",
+        body,
+        needed,
+        args,
+        specs,
+        outs,
+        [pair_columns(o) for o in outs],
+        grid=(width // LANES,),
+        scratch=[pltpu.VMEM((4 * enc, LANES), BF16)] * 3,
+        flops=tok * 2.5 * enc * 20 * 2 * width,
+    )
+
+
+def after_self_attention(place, inputs, ctx_keep, ctx_recv, out_weight, gain_vec, query_weight):
+    tok, width = inputs.shape
+
+    def body(s, in_ref, keep_ref, recv_ref, wk_ref, wr_ref, gain_ref, wq_ref, x_ref, h_ref, q_ref, ctx_ref):
+        total = dot_nn(keep_ref[...], wk_ref[...]) + dot_nn(recv_ref[...], wr_ref[...])
+        residual = in_ref[...].astype(F32) + total
+        x_ref[...] = residual
+        normed = (unit_norm(residual)[0] * gain_ref[...]).astype(BF16)
+        h_ref[...] = normed
+        q_ref[...] = (dot_nn(normed, wq_ref[...]) * SCALE).astype(BF16)
+        ctx_ref[:, pl.ds(pl.multiple_of(s[0] * HALF, LANES), HALF)] = keep_ref[...]
+        ctx_ref[:, pl.ds(pl.multiple_of((1 - s[0]) * HALF, LANES), HALF)] = recv_ref[...]
+
+    args = (inputs, ctx_keep, ctx_recv, out_weight, out_weight, gain_vec, query_weight)
+    specs = [whole(a) for a in args]
+    specs[3] = pl.BlockSpec((HALF, width), lambda _, s: (s[0], 0))
+    specs[4] = pl.BlockSpec((HALF, width), lambda _, s: (1 - s[0], 0))
+    outs = [struct((tok, width), F32)] + [struct((tok, width), BF16)] * 3
+    return run_kernel(
+        "after_self_attention", body, place, args, specs, outs, [whole(o) for o in outs], flops=4 * tok * width * width
+    )
+
+
+def split_rows(total, s, keep_ref, send_ref, write, groups, rows):
+    for at in range(groups):
+        for target, half in ((keep_ref, s[0]), (send_ref, 1 - s[0])):
+            first = pl.multiple_of(at * 2 * rows + half * rows, 16)
+            write(target, at, total[pl.ds(first, rows), :].astype(BF16))
+
+
+def feed_forward(place, residual, context, out_weight, gain_vec, feed_in, feed_out, cotangent):
+    tok, width = residual.shape
+    hidden_width = feed_in.shape[1]
+    steps = 4
+    chunk = hidden_width // steps
+    rows_in = width // 16
+    rows_out = hidden_width // 16
+
+    def body(
+        s, x1_ref, ctx_ref, wo_ref, gain_ref, w1_ref, w2_ref, g_ref,
+        out_ref, dx_ref, low_ref, dctx_ref, gain_grad_ref, keep1, send1, keep2, send2,
+        x2, normed, sum_out, sum_norm, total,
+    ):
+        step = pl.program_id(0)
+
+        @pl.when(step == 0)
+        def _():
+            x2[...] = x1_ref[...] + dot_nn(ctx_ref[...], wo_ref[...])
+            normed[...] = (unit_norm(x2[...])[0] * gain_ref[...]).astype(BF16)
+            sum_out[...] = jnp.zeros_like(sum_out)
+            sum_norm[...] = jnp.zeros_like(sum_norm)
+
+        w1, w2, grad = (w1_ref[...], w2_ref[...], g_ref[...])
+        pre = dot_nn(normed[...], w1)
+        root = 0.7978845608028654
+        bend = 0.044715
+        square = pre * pre
+        swing = jnp.tanh(root * (pre + bend * pre * square))
+        hidden = (0.5 * pre * (1.0 + swing)).astype(BF16)
+        sum_out[...] += dot_nn(hidden, w2)
+        slope = 0.5 * (1.0 + swing) + 0.5 * pre * (1.0 - swing * swing) * (root * (1.0 + 3.0 * bend * square))
+        grad_pre = (dot_nt(grad, w2) * slope).astype(BF16)
+        sum_norm[...] += dot_nt(grad_pre, w1)
+        total[...] = dot_tn(normed[...], grad_pre)
+
+        def write_in(target, at, values):
+            deep, far = (at // 2, at % 2)
+            for unit in range(2):
+                target[0, far, deep % 2, deep // 2, unit] = values[:, unit * HALF : (unit + 1) * HALF]
+
+        split_rows(total, s, keep1, send1, write_in, 8, rows_in)
+        total[...] = dot_tn(hidden, grad)
+
+        def write_out(target, at, values):
+            for side in range(2):
+                target[at, 0, 0, side] = values[:, side * HALF : (side + 1) * HALF]
+
+        split_rows(total, s, keep2, send2, write_out, 2, rows_out)
+
+        @pl.when(step == steps - 1)
+        def _():
+            out_ref[...] = (x2[...] + sum_out[...]).astype(BF16)
+            back, gain_grad_ref[...] = norm_pull(x2[...], gain_ref[...], sum_norm[...])
+            grad_x = grad.astype(F32) + back
+            dx_ref[...] = grad_x
+            low = grad_x.astype(BF16)
+            low_ref[...] = low
+            dctx_ref[...] = dot_nt(low, wo_ref[...]).astype(BF16)
+
+    args = (residual, context, out_weight, gain_vec, feed_in, feed_out, cotangent)
+    specs = [whole(a) for a in args]
+    specs[4] = pl.BlockSpec((width, chunk), lambda c, _: (0, c))
+    specs[5] = pl.BlockSpec((chunk, width), lambda c, _: (c, 0))
+    outs = [
+        struct((tok, width), BF16),
+        struct((tok, width), F32),
+        struct((tok, width), BF16),
+        struct((tok, width), BF16),
+        struct((1, width), F32),
+        struct((2, 2, 2, 2, 4, rows_in, HALF), BF16),
+        struct((2, 2, 2, 2, 4, rows_in, HALF), BF16),
+        struct((2, 2, 2, 2, rows_out, HALF), BF16),
+        struct((2, 2, 2, 2, rows_out, HALF), BF16),
+    ]
+    out_specs = [whole(o) for o in outs]
+    in_block = pl.BlockSpec((1, 2, 2, 2, 2, rows_in, HALF), lambda c, _: (c // 2, 0, 0, 0, c % 2, 0, 0))
+    out_block = pl.BlockSpec((2, 1, 1, 2, rows_out, HALF), lambda c, _: (0, c % 2, c // 2, 0, 0, 0))
+    out_specs[5] = out_specs[6] = in_block
+    out_specs[7] = out_specs[8] = out_block
+    return run_kernel(
+        "feed_forward",
+        body,
+        place,
+        args,
+        specs,
+        outs,
+        out_specs,
+        grid=(steps,),
+        scratch=[
+            pltpu.VMEM((tok, width), F32),
+            pltpu.VMEM((tok, width), BF16),
+            pltpu.VMEM((tok, width), F32),
+            pltpu.VMEM((tok, width), F32),
+            pltpu.VMEM((width, width), F32),
+        ],
+        flops=12 * tok * width * hidden_width + 4 * tok * width * width,
+    )
+
+
+def after_cross_pull(place, residual, grad_res, grad_query, query_weight, gain_vec, out_weight):
+    tok, width = residual.shape
+
+    def body(s, x_ref, dx_ref, dq_ref, wq_ref, gain_ref, wk_ref, wr_ref, dx1_ref, low_ref, gain_grad_ref, keep_ref, send_ref):
+        back, gain_grad_ref[...] = norm_pull(x_ref[...], gain_ref[...], dot_nt(dq_ref[...], wq_ref[...]))
+        grad_x = dx_ref[...] + back
+        dx1_ref[...] = grad_x
+        low = grad_x.astype(BF16)
+        low_ref[...] = low
+        keep_ref[...] = dot_nt(low, wk_ref[...]).astype(BF16)
+        send_ref[...] = dot_nt(low, wr_ref[...]).astype(BF16)
+
+    args = (residual, grad_res, grad_query, query_weight, gain_vec, out_weight, out_weight)
+    specs = [whole(a) for a in args]
+    specs[5] = pl.BlockSpec((HALF, width), lambda _, s: (s[0], 0))
+    specs[6] = pl.BlockSpec((HALF, width), lambda _, s: (1 - s[0], 0))
+    outs = [struct((tok, width), F32), struct((tok, width), BF16), struct((1, width), F32)]
+    outs += [struct((tok, HALF), BF16)] * 2
+    return run_kernel(
+        "after_cross_pull", body, place, args, specs, outs, [whole(o) for o in outs], flops=4 * tok * width * width
+    )
+
+
+def square_grads(name, place, pairs, columns, extra=None):
+    width = pairs[0][0][0].shape[1]
+    rows = width // 16
+    sides = columns // HALF
+    count = len(pairs)
+    extra_rows = 0 if extra is None else 16
+    lefts = [part for left, _ in pairs for part in left]
+    rights = [part for _, right in pairs for part in right]
+    at_left = [sum(len(left) for left, _ in pairs[:m]) for m in range(count)]
+    at_right = [sum(len(right) for _, right in pairs[:m]) for m in range(count)]
+
+    def body(s, *refs):
+        left_refs, right_refs = refs[: len(lefts)], refs[len(lefts) : len(lefts) + len(rights)]
+        rest = refs[len(lefts) + len(rights) :]
+        if extra is not None:
+            extra_ref, rest = rest[0], rest[1:]
+        keep, send, total = rest
+        for m, (left, right) in enumerate(pairs):
+            value = None
+            for a in range(len(left)):
+                left_part = left_refs[at_left[m] + a][...]
+                if len(right) == len(left):
+                    right_part = right_refs[at_right[m] + a][...]
+                else:
+                    right_part = right_refs[at_right[m]][pl.ds(a * left_part.shape[0], left_part.shape[0]), :]
+                part = dot_tn(left_part, right_part)
+                value = part if value is None else value + part
+            total[...] = value
+
+            def write(target, at, values, m=m):
+                deep, far = (at // 2, at % 2)
+                for side in range(sides):
+                    target[far, side, deep % 2, deep // 2, pl.ds(m * rows, rows), :] = values[
+                        :, side * HALF : (side + 1) * HALF
+                    ]
+
+            split_rows(total, s, keep, send, write, 8, rows)
+        if extra is not None:
+            for at in range(8):
+                deep, far = (at // 2, at % 2)
+                row = lax.broadcasted_iota(jnp.int32, (extra_rows, 1), 0)
+                value = jnp.where(row == 0, extra_ref[at : at + 1, :], 0.0).astype(BF16)
+                for target in (keep, send):
+                    for side in range(sides):
+                        target[far, side, deep % 2, deep // 2, pl.ds(count * rows, extra_rows), :] = value
+
+    args = (*lefts, *rights) + (() if extra is None else (extra,))
+    outs = [struct((2, sides, 2, 2, count * rows + extra_rows, HALF), BF16)] * 2
+    return run_kernel(
+        name,
+        body,
+        place,
+        args,
+        [whole(a) for a in args],
+        outs,
+        [whole(o) for o in outs],
+        scratch=[pltpu.VMEM((width, columns), F32)],
+        flops=sum(2 * sum(p.shape[0] for p in left) * width * columns for left, _ in pairs),
+    )
+
+
+def passage_grads(place, grad_keys, grad_values, key_weight, value_weight):
+    keys4, width = grad_keys.shape
+    enc = keys4 // 4
+
+    def body(s, dk_ref, dv_ref, wk_ref, wv_ref, keep_ref, send_ref):
+        for slot in range(4):
+            rows = pl.ds(slot * enc, enc)
+            value = dot_nt(dk_ref[rows, :], wk_ref[...]) + dot_nt(dv_ref[rows, :], wv_ref[...])
+            if slot % 2 == 0:
+                keep_ref[slot // 2] = value
+            else:
+                send_ref[slot // 2] = value.astype(BF16)
+
+    args = (grad_keys, grad_values, key_weight, value_weight)
+    outs = [struct((2, enc, width), F32), struct((2, enc, width), BF16)]
+    return run_kernel(
+        "passage_grads", body, place, args, [whole(a) for a in args], outs, [whole(o) for o in outs],
+        flops=4 * keys4 * width * width,
+    )
+
+
+def normed_grads(name, place, normed, gain_vec, grads, weights):
+    both, width = normed.shape
+    tok = both // 2
+    count = len(grads)
+
+    def body(s, h_ref, gain_ref, *refs):
+        grad_refs, weight_refs = refs[:count], refs[count : 2 * count]
+        keep_ref, send_ref, gain_grad_ref = refs[2 * count :]
+        running = None
+        for target, part in ((keep_ref, s[0]), (send_ref, 1 - s[0])):
+            rows = pl.ds(pl.multiple_of(part * tok, tok), tok)
+            value = None
+            for grad_ref, weight_ref in zip(grad_refs, weight_refs):
+                piece = dot_nt(grad_ref[rows, :], weight_ref[...])
+                value = piece if value is None else value + piece
+            target[...] = value.astype(BF16)
+            inner = jnp.sum(value * h_ref[rows, :].astype(F32), axis=0, keepdims=True)
+            running = inner if running is None else running + inner
+        gain_grad_ref[...] = running / gain_ref[...]
+
+    columns = pl.BlockSpec((width, HALF), lambda _, s: (0, s[0]))
+    args = (normed, gain_vec, *grads, *weights)
+    outs = [struct((tok, width), BF16)] * 2 + [struct((1, width), F32)]
+    return run_kernel(
+        name, body, place, args, [whole(a) for a in args[: 2 + count]] + [columns] * count, outs,
+        [whole(o) for o in outs], flops=4 * tok * width * HALF * count,
+    )
+
+
+def last_pull(place, inputs, gain_vec, grad_res, parts):
+    tok, width = inputs.shape
+
+    def body(s, in_ref, gain_ref, dx_ref, *refs):
+        part_refs, out_ref = refs[:-1], refs[-1]
+        total = part_refs[0][...].astype(F32)
+        for ref in part_refs[1:]:
+            total = total + ref[...].astype(F32)
+        out_ref[...] = dx_ref[...] + norm_pull(in_ref[...].astype(F32), gain_ref[...], total)[0]
+
+    args = (inputs, gain_vec, grad_res, *parts)
+    outs = [struct((tok, width), F32)]
+    return run_kernel(
+        "last_pull", body, place, args, [whole(a) for a in args], outs, [whole(outs[0])], flops=20 * tok * width
+    )[0]
+
+
+def add_split(half, keep, recv):
+    rows = keep.shape[1]
+    steps = 1
+    while rows // steps > 512 and rows % (steps * 2) == 0 and (rows // (steps * 2)) % 16 == 0:
+        steps *= 2
+    tile = rows // steps
+
+    def body(s, km_ref, rm_ref, ko_ref, ro_ref, keep_ref, send_ref):
+        keep_ref[...] = (km_ref[0].astype(F32) + rm_ref[0].astype(F32)).astype(BF16)
+        send_ref[...] = (ko_ref[0].astype(F32) + ro_ref[0].astype(F32)).astype(BF16)
+
+    mine = pl.BlockSpec((1, tile, HALF), lambda i, s: (s[0], i, 0))
+    other = pl.BlockSpec((1, tile, HALF), lambda i, s: (1 - s[0], i, 0))
+    outs = [struct((rows, HALF), BF16)] * 2
+    flat = pl.BlockSpec((tile, HALF), lambda i, s: (i, 0))
+    return run_kernel(
+        "add_split", body, half, (keep, recv, keep, recv), [mine, mine, other, other], outs, [flat, flat], grid=(steps,),
+        flops=4 * rows * HALF,
+    )
+
+
+def sum_over(keep, recv, steps):
+    for half, axis, pairs in steps:
+        kept, send = add_split(half, keep.reshape(2, -1, HALF), recv.reshape(2, -1, HALF))
+        keep, recv = (kept, lax.ppermute(send, axis, pairs))
+    return keep.astype(F32) + recv.astype(F32)
+
+
+def local_paired(
+    inputs,
+    encoded,
+    cotangent,
+    dec_seg,
+    pass_doc,
+    enc_mask,
+    self_query,
+    self_key,
+    self_value,
+    self_output,
+    cross_query,
+    cross_key,
+    cross_value,
+    cross_output,
+    feed_in,
+    feed_out,
+    gain_self,
+    gain_cross,
+    gain_ff,
+):
+    inputs, encoded, cotangent = (inputs[0], encoded[0], cotangent[0])
+    tok, width = inputs.shape
+    enc = encoded.shape[0]
+    blk, row = (lax.axis_index("blk"), lax.axis_index("rows"))
+    core, chip = (blk % 2, blk // 2)
+    y_at, z_low, z_high = (row % 2, (row // 2) % 2, row // 4)
+    place = jnp.stack([core, chip]).astype(jnp.int32)
+    gain_self, gain_cross, gain_ff = (g.reshape(1, width) for g in (gain_self, gain_cross, gain_ff))
+    to_core = lambda array: lax.ppermute(array, "blk", CORE_SWAP)
+    to_chip = lambda array: lax.ppermute(array, "blk", CHIP_SWAP)
+    in_order = lambda mine, other: jnp.where(core == 0, jnp.concatenate([mine, other]), jnp.concatenate([other, mine]))
+
+    def swap(distance):
+        return tuple((at, at ^ distance) for at in range(8))
+
+    one = lambda value: value.astype(jnp.int32).reshape(1)
+    over_x = (one(chip), "blk", CHIP_SWAP)
+    over_y = (one(y_at), "rows", swap(1))
+    over_z = ((one(z_low), "rows", swap(2)), (one(z_high), "rows", swap(4)))
+
+    docs = jnp.where(enc_mask[0] == 1, jnp.broadcast_to(pass_doc[0], (enc,)), -1)
+    spare = 8 * LANES - tok - enc - 1
+    labels = jnp.concatenate([dec_seg[0], docs, pass_doc[0], jnp.zeros((spare,), jnp.int32)]).reshape(8, LANES)
+    labels_x = to_chip(labels)
+    inputs_x = to_chip(inputs)
+    encoded_x = to_chip(encoded)
+    labels = jnp.concatenate([labels, labels_x])
+    labels = jnp.concatenate([labels, to_core(labels)]).reshape(4, 8 * LANES)
+    inputs_c = to_core(inputs)
+    encoded_c = to_core(encoded)
+    seg_own, seg_x, seg_c, seg_d = (labels[at, :tok] for at in range(4))
+    docs_own, docs_x, docs_c, docs_d = (labels[at, tok : tok + enc] for at in range(4))
+
+    lanes = jnp.arange(LANES)[None, :]
+    query_marks = lambda seg: (seg[:, None] == lanes).astype(BF16)
+
+    def key_marks(seg):
+        closed = jnp.where(seg[:, None] != lanes, NEG_FILL, 0.0)
+        return jnp.where(lanes < 3, closed, jnp.where(lanes < 6, 1.0, 0.0)).astype(BF16)
+
+    seg_near, seg_far = (in_order(seg_own, seg_c), in_order(seg_x, seg_d))
+    near_marks, near_keys_marks, far_keys_marks = (query_marks(seg_near), key_marks(seg_near), key_marks(seg_far))
+    own_marks = query_marks(seg_own)
+    doc_marks = (key_marks(jnp.concatenate([docs_own, docs_c])), key_marks(jnp.concatenate([docs_x, docs_d])))
+    slot_docs = jnp.stack([labels[at, tok + enc] for at in (0, 2, 1, 3)])
+    wanted = jnp.any(slot_docs[:, None] == seg_own[None, :], axis=1)
+    count = jnp.sum(wanted.astype(jnp.int32))
+    order = jnp.arange(4)
+    ahead = (order[None, :] < order[:, None]).astype(jnp.int32)
+    before = jnp.sum(ahead * wanted[None, :].astype(jnp.int32), axis=1)
+    spot = jnp.where(wanted, before, count + order - before)
+    listed = jnp.sum(jnp.where(spot[None, :] == order[:, None], order[None, :], 0), axis=1)
+    needed = jnp.concatenate([listed, count[None]]).astype(jnp.int32)
+
+    h1, sq, sk, sv = projections(
+        "near_projections", place, inputs, inputs_c, gain_self, (self_query, self_key, self_value), (SCALE, 1.0, 1.0)
+    )
+    near_out, near_sum = near_attention(place, sq, sk, sv, near_marks, near_keys_marks)
+    ck0, cv0 = passage_pair(place, encoded, encoded_c, cross_key, cross_value)
+    inputs_d = to_core(inputs_x)
+    encoded_d = to_core(encoded_x)
+    h1_far, fk, fv = projections(
+        "far_projections", place, inputs_x, inputs_d, gain_self, (self_key, self_value), (1.0, 1.0)
+    )
+    self_out, self_sum, ctx_keep, ctx_send = far_attention(
+        place, sq, fk, fv, near_marks, far_keys_marks, near_out, near_sum
+    )
+    ck1, cv1 = passage_pair(place, encoded_x, encoded_d, cross_key, cross_value)
+    x1, h2, cq, self_context = after_self_attention(
+        place, inputs, ctx_keep, to_core(ctx_send), self_output, gain_cross, cross_query
+    )
+    cross_context, cross_out, cross_sum = cross_attention(needed, cq, (ck0, ck1), (cv0, cv1), own_marks, doc_marks)
+    output, dx2, e2, d_cross, grad_gain_ff, keep1, send1, keep2, send2 = feed_forward(
+        place, x1, cross_context, cross_output, gain_ff, feed_in, feed_out, cotangent
+    )
+    recv1, recv2 = (to_core(send1), to_core(send2))
+    dcq, dck, dcv = cross_pull(
+        needed, cq, (ck0, ck1), (cv0, cv1), own_marks, doc_marks, d_cross, cross_out, cross_sum
+    )
+    total1 = sum_over(keep1, recv1, (over_x, over_y) + over_z)
+    total2 = sum_over(keep2, recv2, (over_y,) + over_z + (over_x,))
+    dx1, e1, grad_gain_cross, ds_keep, ds_send = after_cross_pull(
+        place, x1, dx2, dcq, cross_query, gain_cross, self_output
+    )
+    ds_recv = to_core(ds_send)
+    dq_far, dk_far, dv_far = self_pull(
+        "far_pull", place, False, sq, fk, fv, near_marks, far_keys_marks, ds_keep, ds_recv, self_out, self_sum,
+        jnp.zeros((8, LANES), F32),
+    )
+    far_keep, far_send, gain_far = normed_grads(
+        "far_normed_grads", place, h1_far, gain_self, (dk_far, dv_far), (self_key, self_value)
+    )
+    far_here = (far_keep.astype(F32) + to_core(far_send).astype(F32)).astype(BF16)
+    from_far = to_chip(far_here)
+    enc_keep, enc_send = passage_grads(place, dck, dcv, cross_key, cross_value)
+    enc_sum = enc_keep + to_core(enc_send).astype(F32)
+    encoded_grad = enc_sum[0] + to_chip(enc_sum[1].astype(BF16)).astype(F32)
+    passages = (encoded, encoded_c, encoded_x, encoded_d)
+    keep3, send3 = square_grads(
+        "cross_grads",
+        place,
+        (
+            ((cross_context,), (e2,)),
+            ((h2,), (dcq,)),
+            (passages, (dck,)),
+            (passages, (dcv,)),
+            ((self_context,), (e1,)),
+        ),
+        width,
+    )
+    total3 = sum_over(keep3, to_core(send3), (over_y, over_x) + over_z)
+    dq, dk, dv = self_pull(
+        "near_pull", place, True, sq, sk, sv, near_marks, near_keys_marks, ds_keep, ds_recv, self_out, self_sum, dq_far
+    )
+    near_keep, near_send, gain_near = normed_grads(
+        "near_normed_grads", place, h1, gain_self, (dq, dk, dv), (self_query, self_key, self_value)
+    )
+    input_grad = last_pull(place, inputs, gain_self, dx1, (near_keep, to_core(near_send), from_far))
+    gains = jnp.concatenate([gain_far + gain_near, grad_gain_cross, grad_gain_ff])
+    gains = gains + to_core(gains)
+    gains = jnp.transpose(gains.reshape(3, 8, width // 8), (1, 0, 2)).reshape(8, 3 * (width // 8))
+    gains = jnp.pad(gains, ((0, 0), (0, HALF - gains.shape[1])))
+    keep4, send4 = square_grads(
+        "self_grads",
+        place,
+        (((h1,), (dq,)), ((h1, h1_far), (dk, dk_far)), ((h1, h1_far), (dv, dv_far))),
+        HALF,
+        gains,
+    )
+    recv4 = to_core(send4)
+    here = chip == core
+    keep4, send4 = (jnp.where(here, keep4, recv4), jnp.where(here, recv4, keep4))
+    total4 = sum_over(keep4, to_chip(send4), (over_y,) + over_z)
+
+    wide = total1.reshape(4, width // 16, HALF)
+    wide_keep = lax.dynamic_slice_in_dim(wide, 2 * core, 2)
+    wide_recv = to_core(lax.dynamic_slice_in_dim(wide, 2 * (1 - core), 2))
+    side = HALF // 2
+    rows = width // 16
+    tall = total2.shape[0]
+    rest = jnp.concatenate([total2, total3, total4[: 3 * rows]])
+    rest_keep = jnp.where(core == 0, rest[:, :side], rest[:, side:])
+    rest_recv = to_core(jnp.where(core == 0, rest[:, side:], rest[:, :side]))
+    join = lambda array: jnp.transpose(array, (1, 0, 2)).reshape(rows, 2 * HALF)
+    grad_feed_in = in_order(join(wide_keep), join(wide_recv))
+    grad_feed_out = in_order(rest_keep[:tall], rest_recv[:tall])
+    squares = []
+    for at in range(8):
+        part = slice(tall + at * rows, tall + (at + 1) * rows)
+        squares.append(in_order(rest_keep[part], rest_recv[part]))
+    cross_o, cross_q, cross_k, cross_v, self_o, self_q, self_k, self_v = squares
+    gain_row = total4[3 * rows]
+    piece = width // 8
+    return (
+        output[None],
+        input_grad[None],
+        encoded_grad[None],
+        self_q,
+        self_k,
+        self_v,
+        self_o,
+        cross_q,
+        cross_k,
+        cross_v,
+        cross_o,
+        grad_feed_in,
+        grad_feed_out,
+        gain_row[:piece],
+        gain_row[piece : 2 * piece],
+        gain_row[2 * piece : 3 * piece],
+    )
+
+
 def solution(mesh):
+    paired = mesh.shape["blk"] == 4 and mesh.shape["rows"] == 8
+    body = local_paired if paired else local_any
     in_specs = (
         P("rows", "blk", None),
         P("rows", "blk", None),
@@ -387,4 +1322,4 @@
         P("rows"),
         P("rows"),
     )
-    return jax.shard_map(local, mesh=mesh, in_specs=in_specs, out_specs=out_specs, check_vma=False)
+    return jax.shard_map(body, mesh=mesh, in_specs=in_specs, out_specs=out_specs, check_vma=False)

time: 1710 us -> 430 us (0.25)
  waiting for transfers between devices: 1110 us -> 86.9 us
  matrix products: 335 us -> 0 us
  Pallas kernels: 0 us -> 238 us
  local copies, waits for them, and re-layouts: 93.1 us -> 18.6 us
  other arithmetic: 85.9 us -> 25.6 us
  blocking collectives: 52.4 us -> 0 us
  starting transfers between devices: 1.13 us -> 53.5 us
    reduce_scatter x12 -> x0, waiting for transfers between devices: 1070 us -> none  [the longest x1 142 us: local(): lax.psum_scatter(spread_mats[9], ('rows', 'blk'), scatter_dimension=0, ti...]
    dot_general x74 -> x0, matrix products: 335 us -> none  [the longest x10 75.4 us: head_scores(): jnp.einsum('rqhe,rkhe->rhqk', split_heads(queries), split_heads(keys), pr...]
    pallas_call x0 -> x34, Pallas kernels: none -> 238 us  [run_kernel(): pl.pallas_call(body, grid_spec=pltpu.PrefetchScalarGridSpec(num_scalar_pr...]
    ppermute x0 -> x38, waiting for transfers between devices: none -> 86.9 us  [the longest x15 59 us: sum_over(): keep, recv = (kept, lax.ppermute(send, axis, pairs))]
    ppermute x0 -> x38, starting transfers between devices: none -> 53.5 us  [the longest x6 28.4 us: local_paired(): to_chip = lambda array: lax.ppermute(array, 'blk', CHIP_SWAP)]
    unnamed x2 -> x0, blocking collectives: 47.2 us -> none
    reduce_sum x6 -> x3, other arithmetic: 39 us -> 0.86 us  [the longest x1 0.63 us: local_paired(): count = jnp.sum(wanted.astype(jnp.int32))]
    all_gather x4 -> x0, waiting for transfers between devices: 36.4 us -> none  [the longest x1 24.2 us: local(): piece_keys = lax.all_gather(self_keys, 'blk', axis=1, tiled=True)]
  transfers between devices with their start and end apart: 16 -> 38, of which waited for: 13 -> 11; matrix products, arithmetic and copies ran while one was open for 16% -> 7% of each run, Pallas kernels for 0% -> 44%
where the time goes in v1:
time: 430 us; the launch traced here: 425 us
  Pallas kernels  238 us (55%)
  waiting for transfers between devices  86.9 us (20%)
  starting transfers between devices  53.5 us (12%)
  other arithmetic  25.6 us (6%)
  local copies, waits for them, and re-layouts  18.6 us (4%)
    pallas_call x34, Pallas kernels, run_kernel(): pl.pallas_call(body, grid_spec=pltpu.PrefetchScalarGridSpec(num_scalar_pr...  238 us
    ppermute x15, waiting for transfers between devices, sum_over(): keep, recv = (kept, lax.ppermute(send, axis, pairs))  59 us
    ppermute x6, starting transfers between devices, local_paired(): to_chip = lambda array: lax.ppermute(array, 'blk', CHIP_SWAP)  28.4 us
    ppermute x6, waiting for transfers between devices, local_paired(): to_chip = lambda array: lax.ppermute(array, 'blk', CHIP_SWAP)  24.8 us
    ppermute x15, starting transfers between devices, sum_over(): keep, recv = (kept, lax.ppermute(send, axis, pairs))  21.5 us
    unnamed x63, local copies, waits for them, and re-layouts  10.6 us
  transfers between devices with their start and end apart: 38, of which 11 were waited for; matrix products, arithmetic and copies ran while one was open for 7% of the time, Pallas kernels for 44%

profile of v1, /device:TPU:0, one launch (start us, length us, event | category | flops | bytes accessed | tf_op | source)
XLA Modules:
  0.0 424.6 jit_solution(5219088997157505741)
XLA Ops:
  7.9 24.8 %collective-permute-done.3 = s32[8,128]{1,0:T(8,128)S(1)} collective-permute-done((s32[8,128]{1,0:T(8,128)S(1)}, s32[8,128]{1,0:T(8,128)S(1)}, u32[]{:S(2)}, u32[]{:S(2)}) %collective-permute-start.3) | collective-permute-done | bytes 4128 | tf_op jit(solution)/shard_map/ppermute | solution.py:1119
  47.7 5.8 %near_projections.1 = (bf16[896,768]{1,0:T(8,128)(2,1)}, bf16[896,384]{1,0:T(8,128)(2,1)}, bf16[896,384]{1,0:T(8,128)(2,1)}, bf16[896,384]{1,0:T(8,128)(2,1)}) custom-call(s32[2]{0:T(128)} %pad_add_fusion.4.s, bf16[448,768]{1,0:T(8,128)(2,1)} %bitcast.107, bf16[448,768]{1,0:T(8,128)(2,1)} %copy-done.20, f32[1,768]{1,0:T(1,128)} %reshape.268.gain_ref, ...), custom_call_target="tpu_custom_call" | custom-call | flops 1585446912 | bytes 8358912 | tf_op jit(solution)/shard_map/near_projections/pallas_call | solution.py:384
  53.5 14.7 %near_attention.1 = (f32[896,384]{1,0:T(8,128)}, f32[896,384]{1,0:T(8,128)}) custom-call(s32[2]{0:T(128)} %pad_add_fusion.4.s, bf16[896,384]{1,0:T(8,128)(2,1)} %get-tuple-element.105.q_ref, bf16[896,384]{1,0:T(8,128)(2,1)} %get-tuple-element.108.k_ref, bf16[896,384]{1,0:T(8,128)(2,1)} %get-tuple-element.109.v_ref, bf16[896,128]{1,0:T(8,128)(2,1)} %fusion.3.m_ref, ...), custom_call_target="tpu_custom_call" | custom-call | flops 3699376128 | bytes 5275648 | tf_op jit(solution)/shard_map/near_attention/pallas_call | solution.py:384
  74.0 6.2 %far_attention.1 = (f32[896,384]{1,0:T(8,128)}, f32[896,384]{1,0:T(8,128)}, bf16[448,384]{1,0:T(8,128)(2,1)}, bf16[448,384]{1,0:T(8,128)(2,1)}) custom-call(s32[2]{0:T(128)} %pad_add_fusion.4.s, bf16[896,384]{1,0:T(8,128)(2,1)} %get-tuple-element.105.q_ref, bf16[896,384]{1,0:T(8,128)(2,1)} %get-tuple-element.106.k_ref, ...), custom_call_target="tpu_custom_call" | custom-call | flops 4932501504 | bytes 8716288 | tf_op jit(solution)/shard_map/far_attention/pallas_call | solution.py:384
  82.7 5.7 %passage_pair.2 = (bf16[768,768]{1,0:T(8,128)(2,1)}, bf16[768,768]{1,0:T(8,128)(2,1)}) custom-call(s32[2]{0:T(128)} %pad_add_fusion.4.s, bf16[384,768]{1,0:T(8,128)(2,1)} %bitcast.148, bf16[384,768]{1,0:T(8,128)(2,1)} %copy-done.23, bf16[768,768]{1,0:T(8,128)(2,1)} %wk_ref.5, bf16[768,768]{1,0:T(8,128)(2,1)} %wv_ref.1), custom_call_target="tpu_custom_call" | custom-call | flops 1811939328 | bytes 5898240 | tf_op jit(solution)/shard_map/passage_pair/pallas_call | solution.py:384
  89.2 5.8 %passage_pair.3 = (bf16[768,768]{1,0:T(8,128)(2,1)}, bf16[768,768]{1,0:T(8,128)(2,1)}) custom-call(s32[2]{0:T(128)} %pad_add_fusion.4.s, bf16[384,768]{1,0:T(8,128)(2,1)} %copy-done.22, bf16[384,768]{1,0:T(8,128)(2,1)} %copy-done.24, bf16[768,768]{1,0:T(8,128)(2,1)} %wk_ref.5, bf16[768,768]{1,0:T(8,128)(2,1)} %wv_ref.1), custom_call_target="tpu_custom_call" | custom-call | flops 1811939328 | bytes 5898240 | tf_op jit(solution)/shard_map/passage_pair/pallas_call | solution.py:384
  95.8 5.7 %after_self_attention.1 = (f32[448,768]{1,0:T(8,128)}, bf16[448,768]{1,0:T(8,128)(2,1)}, bf16[448,768]{1,0:T(8,128)(2,1)}, bf16[448,768]{1,0:T(8,128)(2,1)}) custom-call(s32[2]{0:T(128)} %pad_add_fusion.4.s, bf16[448,768]{1,0:T(8,128)(2,1)} %bitcast.108, bf16[448,384]{1,0:T(8,128)(2,1)} %get-tuple-element.112.keep_ref, bf16[448,384]{1,0:T(8,128)(2,1)} %copy-done.12, ...), custom_call_target="tpu_custom_call" | custom-call | flops 1056964608 | bytes 8358912 | tf_op jit(solution)/shard_map/after_self_attention/pallas_call | solution.py:384
  101.5 18.0 %cross_attention.1 = (bf16[448,768]{1,0:T(8,128)(2,1)}, f32[448,768]{1,0:T(8,128)}, f32[448,768]{1,0:T(8,128)}) custom-call(s32[5]{0:T(128)} %pad_add_fusion.6.s, bf16[448,768]{1,0:T(8,128)(2,1)} %get-tuple-element.115.q_ref, bf16[768,768]{1,0:T(8,128)(2,1)} %get-tuple-element.116.k0_ref, bf16[768,768]{1,0:T(8,128)(2,1)} %get-tuple-element.117.k1_ref, ...), custom_call_target="tpu_custom_call" | custom-call | flops 5284823040 | bytes 9355264 | tf_op jit(solution)/shard_map/cross_attention/pallas_call | solution.py:384
  119.5 25.6 %feed_forward.1 = (bf16[448,768]{1,0:T(8,128)(2,1)}, f32[448,768]{1,0:T(8,128)}, bf16[448,768]{1,0:T(8,128)(2,1)}, bf16[448,768]{1,0:T(8,128)(2,1)}, f32[1,768]{...) custom-call(s32[2]{0:T(128)} %pad_add_fusion.4.s, ...), custom_call_target="tpu_custom_call" | custom-call | flops 13740539904 | bytes 26253312 | tf_op jit(solution)/shard_map/feed_forward/pallas_call | solution.py:384
  145.1 24.6 %cross_pull.1 = (bf16[448,768]{1,0:T(8,128)(2,1)}, bf16[1536,768]{1,0:T(8,128)(2,1)}, bf16[1536,768]{1,0:T(8,128)(2,1)}) custom-call(s32[5]{0:T(128)} %pad_add_fusion.6.s, bf16[448,768]{1,0:T(8,128)(2,1)} %get-tuple-element.115.q_ref, bf16[768,768]{1,0:T(8,128)(2,1)} %get-tuple-element.116.k0_ref, bf16[768,768]{1,0:T(8,128)(2,1)} %get-tuple-element.117.k1_ref, ...), custom_call_target="tpu_custom_call" | custom-call | flops 13212057600 | bytes 14761984 | tf_op jit(solution)/shard_map/cross_pull/pallas_call | solution.py:384
  169.7 6.2 %after_cross_pull.1 = (f32[448,768]{1,0:T(8,128)}, bf16[448,768]{1,0:T(8,128)(2,1)}, f32[1,768]{1,0:T(1,128)}, bf16[448,384]{1,0:T(8,128)(2,1)}, bf16[448,384]{1,0:T(8,128)(2,1)}) custom-call(s32[2]{0:T(128)} %pad_add_fusion.4.s, f32[448,768]{1,0:T(8,128)} %get-tuple-element.114.x1_ref.x_ref, f32[448,768]{1,0:T(8,128)} %get-tuple-element.122.dx_ref, ...), custom_call_target="tpu_custom_call" | custom-call | flops 1056964608 | bytes 9738240 | tf_op jit(solution)/shard_map/after_cross_pull/pallas_call | solution.py:384
  176.0 16.0 %cross_grads.1 = (bf16[2,2,2,2,240,384]{5,4,3,2,1,0:T(8,128)(2,1)}, bf16[2,2,2,2,240,384]{5,4,3,2,1,0:T(8,128)(2,1)}) custom-call(s32[2]{0:T(128)} %pad_add_fusion.4.s, bf16[448,768]{1,0:T(8,128)(2,1)} %get-tuple-element.120.ctx_ref.refs_0_, bf16[448,768]{1,0:T(8,128)(2,1)} %get-tuple-element.158.refs_1_, bf16[384,768]{1,0:T(8,128)(2,1)} %bitcast.149, ...), custom_call_target="tpu_custom_call" | custom-call | flops 5209325568 | bytes 19464192 | tf_op jit(solution)/shard_map/cross_grads/pallas_call | solution.py:384
  193.2 6.2 %far_pull.1 = (f32[896,384]{1,0:T(8,128)}, bf16[896,384]{1,0:T(8,128)(2,1)}, bf16[896,384]{1,0:T(8,128)(2,1)}) custom-call(s32[2]{0:T(128)} %pad_add_fusion.4.s, bf16[896,384]{1,0:T(8,128)(2,1)} %get-tuple-element.105.q_ref, bf16[896,384]{1,0:T(8,128)(2,1)} %get-tuple-element.106.k_ref, bf16[896,384]{1,0:T(8,128)(2,1)} %get-tuple-element.107.v_ref, ...), custom_call_target="tpu_custom_call" | custom-call | flops 12331253760 | bytes 8720384 | tf_op jit(solution)/shard_map/far_pull/pallas_call | solution.py:384
  199.4 16.0 %near_pull.1 = (bf16[896,384]{1,0:T(8,128)(2,1)}, bf16[896,384]{1,0:T(8,128)(2,1)}, bf16[896,384]{1,0:T(8,128)(2,1)}) custom-call(s32[2]{0:T(128)} %pad_add_fusion.4.s, bf16[896,384]{1,0:T(8,128)(2,1)} %get-tuple-element.105.q_ref, bf16[896,384]{1,0:T(8,128)(2,1)} %get-tuple-element.108.k_ref, bf16[896,384]{1,0:T(8,128)(2,1)} %get-tuple-element.109.v_ref, ...), custom_call_target="tpu_custom_call" | custom-call | flops 9248440320 | bytes 9404416 | tf_op jit(solution)/shard_map/near_pull/pallas_call | solution.py:384
  215.4 6.5 %near_normed_grads.1 = (bf16[448,768]{1,0:T(8,128)(2,1)}, bf16[448,768]{1,0:T(8,128)(2,1)}, f32[1,768]{1,0:T(1,128)}) custom-call(s32[2]{0:T(128)} %pad_add_fusion.4.s, bf16[896,768]{1,0:T(8,128)(2,1)} %get-tuple-element.128.h_ref.refs_0_.refs_1_.refs_3_, f32[1,768]{1,0:T(1,128)} %reshape.268.gain_ref, bf16[896,384]{1,0:T(8,128)(2,1)} %get-tuple-element.134.refs_0_.refs_5_, ...), custom_call_target="tpu_custom_call" | custom-call | flops 1585446912 | bytes 8361984 | tf_op jit(solution)/shard_map/near_normed_grads/pallas_call | solution.py:384
  230.1 10.4 %self_grads.1 = (bf16[2,1,2,2,160,384]{5,4,3,2,1,0:T(8,128)(2,1)}, bf16[2,1,2,2,160,384]{5,4,3,2,1,0:T(8,128)(2,1)}) custom-call(s32[2]{0:T(128)} %pad_add_fusion.4.s, bf16[896,768]{1,0:T(8,128)(2,1)} %get-tuple-element.128.h_ref.refs_0_.refs_1_.refs_3_, bf16[896,768]{1,0:T(8,128)(2,1)} %get-tuple-element.128.h_ref.refs_0_.refs_1_.refs_3_, ...), custom_call_target="tpu_custom_call" | custom-call | flops 2642411520 | bytes 12300288 | tf_op jit(solution)/shard_map/self_grads/pallas_call | solution.py:384
  246.1 22.3 %collective-permute-start.27 = (bf16[2,1,2,2,160,384]{5,4,3,2,1,0:T(8,128)(2,1)S(1)}, bf16[2,1,2,2,160,384]{5,4,3,2,1,0:T(8,128)(2,1)}, u32[]{:S(2)}, u32[]{:S(2)}) collective-permute-start(bf16[2,1,2,2,160,384]{5,4,3,2,1,0:T(8,128)(2,1)S(1)} %get-tuple-element.262), channel_id=1, source_target_pairs={{0,2},{2,0},{1,3},{3,1},{4,6},{6,4},{5,7},{7,5},{8,10},{10,8},{9,1... | collective-permute-start | bytes 2949128 | tf_op jit(solution)/shard_map/ppermute | solution.py:1119
  268.4 8.7 %passage_grads.1 = (f32[2,384,768]{2,1,0:T(8,128)}, bf16[2,384,768]{2,1,0:T(8,128)(2,1)}) custom-call(s32[2]{0:T(128)} %pad_add_fusion.4.s, bf16[1536,768]{1,0:T(8,128)(2,1)} %get-tuple-element.144.dk_ref.refs_13_, bf16[1536,768]{1,0:T(8,128)(2,1)} %get-tuple-element.145.dv_ref.refs_14_, bf16[768,768]{1,0:T(8,128)(2,1)} %wk_ref.5, bf16[768,768]{1,0:T(8,128)(2,1)} %wv_ref.1), custom_call_target="tpu_custom_call" | custom-call | flops 3623878656 | bytes 10616832 | tf_op jit(solution)/shard_map/passage_grads/pallas_call | solution.py:384
  301.2 9.5 %collective-permute-done.16 = bf16[1536,384]{1,0:T(8,128)(2,1)} collective-permute-done((bf16[1536,384]{1,0:T(8,128)(2,1)}, bf16[1536,384]{1,0:T(8,128)(2,1)}, u32[]{:S(2)}, u32[]{:S(2)}) %collective-permute-start.16) | collective-permute-done | bytes 1179680 | tf_op jit(solution)/shard_map/ppermute | solution.py:1085
  316.2 6.8 %collective-permute-done.33 = bf16[1536,384]{1,0:T(8,128)(2,1)S(1)} collective-permute-done((bf16[1536,384]{1,0:T(8,128)(2,1)}, bf16[1536,384]{1,0:T(8,128)(2,1)S(1)}, u32[]{:S(2)}, u32[]{:S(2)}) %collective-permute-start.33) | collective-permute-done | bytes 1179680 | tf_op jit(solution)/shard_map/ppermute | solution.py:1085
  328.5 13.7 %collective-permute-done.21 = bf16[1920,384]{1,0:T(8,128)(2,1)} collective-permute-done((bf16[1920,384]{1,0:T(8,128)(2,1)}, bf16[1920,384]{1,0:T(8,128)(2,1)}, u32[]{:S(2)}, u32[]{:S(2)}) %collective-permute-start.21) | collective-permute-done | bytes 1474592 | tf_op jit(solution)/shard_map/ppermute | solution.py:1085
  345.4 7.5 %collective-permute-done.28 = bf16[640,384]{1,0:T(8,128)(2,1)} collective-permute-done((bf16[640,384]{1,0:T(8,128)(2,1)}, bf16[640,384]{1,0:T(8,128)(2,1)}, u32[]{:S(2)}, u32[]{:S(2)}) %collective-permute-start.28) | collective-permute-done | bytes 491552 | tf_op jit(solution)/shard_map/ppermute | solution.py:1085
  375.6 9.3 %collective-permute-done.35 = bf16[384,384]{1,0:T(8,128)(2,1)S(1)} collective-permute-done((bf16[384,384]{1,0:T(8,128)(2,1)}, bf16[384,384]{1,0:T(8,128)(2,1)S(1)}, u32[]{:S(2)}, u32[]{:S(2)}) %collective-permute-start.35) | collective-permute-done | bytes 294944 | tf_op jit(solution)/shard_map/ppermute | solution.py:1085
  405.6 10.4 %collective-permute-done.24 = bf16[240,384]{1,0:T(8,128)(2,1)S(1)} collective-permute-done((bf16[240,384]{1,0:T(8,128)(2,1)}, bf16[240,384]{1,0:T(8,128)(2,1)S(1)}, u32[]{:S(2)}, u32[]{:S(2)}) %collective-permute-start.24) | collective-permute-done | bytes 184352 | tf_op jit(solution)/shard_map/ppermute | solution.py:1085
  (215 shorter events, 135.8 us)
Async XLA Ops:
  0.6 46.1 %collective-permute-start = (bf16[448,768]{1,0:T(8,128)(2,1)}, bf16[448,768]{1,0:T(8,128)(2,1)S(1)}, u32[]{:S(2)}, u32[]{:S(2)}) collective-permute-start(bf16[448,768]{1,0:T(8,128)(2,1)} %bitcast.105), channel_id=1, source_target_pairs={{0,1},{1,0},{2,3},{3,2},{4,5},{5,4},{6,7},{7,6},{8,9},{9,8},{10,11... | collective-permute-start | bytes 2064392 | tf_op jit(solution)/shard_map/ppermute | solution.py:1118
  1.2 44.2 %collective-permute-start.1 = (bf16[448,768]{1,0:T(8,128)(2,1)}, bf16[448,768]{1,0:T(8,128)(2,1)S(1)}, u32[]{:S(2)}, u32[]{:S(2)}) collective-permute-start(bf16[448,768]{1,0:T(8,128)(2,1)} %bitcast.106), channel_id=1, source_target_pairs={{0,2},{2,0},{1,3},{3,1},{4,6},{6,4},{5,7},{7,5},{8,10},{10,8},{9,1... | collective-permute-start | bytes 2064392 | tf_op jit(solution)/shard_map/ppermute | solution.py:1119
  3.7 42.9 %collective-permute-start.7 = (bf16[384,768]{1,0:T(8,128)(2,1)}, bf16[384,768]{1,0:T(8,128)(2,1)S(1)}, u32[]{:S(2)}, u32[]{:S(2)}) collective-permute-start(bf16[384,768]{1,0:T(8,128)(2,1)} %bitcast.146), channel_id=1, source_target_pairs={{0,2},{2,0},{1,3},{3,1},{4,6},{6,4},{5,7},{7,5},{8,10},{10,8},{9,1... | collective-permute-start | bytes 1769480 | tf_op jit(solution)/shard_map/ppermute | solution.py:1119
  3.8 78.0 %collective-permute-start.6 = (bf16[384,768]{1,0:T(8,128)(2,1)}, bf16[384,768]{1,0:T(8,128)(2,1)S(1)}, u32[]{:S(2)}, u32[]{:S(2)}) collective-permute-start(bf16[384,768]{1,0:T(8,128)(2,1)} %bitcast.147), channel_id=1, source_target_pairs={{0,1},{1,0},{2,3},{3,2},{4,5},{5,4},{6,7},{7,6},{8,9},{9,8},{10,11... | collective-permute-start | bytes 1769480 | tf_op jit(solution)/shard_map/ppermute | solution.py:1118
  6.0 26.7 %collective-permute-start.3 = (s32[8,128]{1,0:T(8,128)S(1)}, s32[8,128]{1,0:T(8,128)S(1)}, u32[]{:S(2)}, u32[]{:S(2)}) collective-permute-start(s32[8,128]{1,0:T(8,128)S(1)} %add_bitcast_fusion), channel_id=1, source_target_pairs={{0,2},{2,0},{1,3},{3,1},{4,6},{6,4},{5,7},{7,5},{8,10},{10,8},{9,1... | collective-permute-start | bytes 12296 | tf_op jit(solution)/shard_map/ppermute | solution.py:1119
  45.4 22.9 %collective-permute-start.2 = (bf16[448,768]{1,0:T(8,128)(2,1)S(1)}, bf16[448,768]{1,0:T(8,128)(2,1)S(1)}, u32[]{:S(2)}, u32[]{:S(2)}) collective-permute-start(bf16[448,768]{1,0:T(8,128)(2,1)S(1)} %collective-permute-done.1.mine_ref), channel_id=1, source_target_pairs={{0,1},{1,0},{2,3},{3,2},{4,5},{5,4},{6,7},{7,6},{8,9},{9,8},{10,11... | collective-permute-start | bytes 2064392 | tf_op jit(solution)/shard_map/ppermute | solution.py:1118
  46.6 41.8 %collective-permute-start.8 = (bf16[384,768]{1,0:T(8,128)(2,1)S(1)}, bf16[384,768]{1,0:T(8,128)(2,1)S(1)}, u32[]{:S(2)}, u32[]{:S(2)}) collective-permute-start(bf16[384,768]{1,0:T(8,128)(2,1)S(1)} %collective-permute-done.7.first_ref.refs_4_.refs_8_), channel_id=1, source_target_pairs={{0,1},{1,0},{2,3},{3,2},{4,5},{5,4},{6,7},{7,6},{8,9},{9,8},{10,11... | collective-permute-start | bytes 1769480 | tf_op jit(solution)/shard_map/ppermute | solution.py:1118
  145.1 132.1 %collective-permute-start.15 = (bf16[2,2,2,2,192,384]{5,4,3,2,1,0:T(8,128)(2,1)}, bf16[2,2,2,2,192,384]{5,4,3,2,1,0:T(8,128)(2,1)}, u32[]{:S(2)}, u32[]{:S(2)}) collective-permute-start(bf16[2,2,2,2,192,384]{5,4,3,2,1,0:T(8,128)(2,1)} %get-tuple-element.149), channel_id=1, source_target_pairs={{0,1},{1,0},{2,3},{3,2},{4,5},{5,4},{6,7},{7,6},{8,9},{9,8},{10,11... | collective-permute-start | bytes 7077896 | tf_op jit(solution)/shard_map/ppermute | solution.py:1118
  191.9 89.6 %collective-permute-start.20 = (bf16[2,2,2,2,240,384]{5,4,3,2,1,0:T(8,128)(2,1)}, bf16[2,2,2,2,240,384]{5,4,3,2,1,0:T(8,128)(2,1)S(1)}, u32[]{:S(2)}, u32[]{:S(2)}) collective-permute-start(bf16[2,2,2,2,240,384]{5,4,3,2,1,0:T(8,128)(2,1)} %get-tuple-element.163), channel_id=1, source_target_pairs={{0,1},{1,0},{2,3},{3,2},{4,5},{5,4},{6,7},{7,6},{8,9},{9,8},{10,11... | collective-permute-start | bytes 8847368 | tf_op jit(solution)/shard_map/ppermute | solution.py:1118
  228.2 59.8 %collective-permute-start.32 = (bf16[2,2,2,2,4,48,384]{6,5,4,3,2,1,0:T(8,128)(2,1)}, bf16[2,2,2,2,4,48,384]{6,5,4,3,2,1,0:T(8,128)(2,1)}, u32[]{:S(2)}, u32[]{:S(2)}) collective-permute-start(bf16[2,2,2,2,4,48,384]{6,5,4,3,2,1,0:T(8,128)(2,1)} %get-tuple-element.185), channel_id=1, source_target_pairs={{0,1},{1,0},{2,3},{3,2},{4,5},{5,4},{6,7},{7,6},{8,9},{9,8},{10,11... | collective-permute-start | bytes 7077896 | tf_op jit(solution)/shard_map/ppermute | solution.py:1118
  240.7 53.2 %collective-permute-start.11 = (bf16[448,768]{1,0:T(8,128)(2,1)}, bf16[448,768]{1,0:T(8,128)(2,1)S(1)}, u32[]{:S(2)}, u32[]{:S(2)}) collective-permute-start(bf16[448,768]{1,0:T(8,128)(2,1)} %get-tuple-element.143), channel_id=1, source_target_pairs={{0,1},{1,0},{2,3},{3,2},{4,5},{5,4},{6,7},{7,6},{8,9},{9,8},{10,11... | collective-permute-start | bytes 2064392 | tf_op jit(solution)/shard_map/ppermute | solution.py:1118
  246.1 48.2 %collective-permute-start.27 = (bf16[2,1,2,2,160,384]{5,4,3,2,1,0:T(8,128)(2,1)S(1)}, bf16[2,1,2,2,160,384]{5,4,3,2,1,0:T(8,128)(2,1)}, u32[]{:S(2)}, u32[]{:S(2)}) collective-permute-start(bf16[2,1,2,2,160,384]{5,4,3,2,1,0:T(8,128)(2,1)S(1)} %get-tuple-element.262), channel_id=1, source_target_pairs={{0,2},{2,0},{1,3},{3,1},{4,6},{6,4},{5,7},{7,5},{8,10},{10,8},{9,1... | collective-permute-start | bytes 2949128 | tf_op jit(solution)/shard_map/ppermute | solution.py:1119
  281.5 29.2 %collective-permute-start.16 = (bf16[1536,384]{1,0:T(8,128)(2,1)}, bf16[1536,384]{1,0:T(8,128)(2,1)}, u32[]{:S(2)}, u32[]{:S(2)}) collective-permute-start(bf16[1536,384]{1,0:T(8,128)(2,1)} %get-tuple-element.151), channel_id=1, source_target_pairs={{0,4},{4,0},{8,12},{12,8},{16,20},{20,16},{24,28},{28,24},{1,5},{5... | collective-permute-start | bytes 3538952 | tf_op jit(solution)/shard_map/ppermute | solution.py:1085
  287.9 54.3 %collective-permute-start.21 = (bf16[1920,384]{1,0:T(8,128)(2,1)}, bf16[1920,384]{1,0:T(8,128)(2,1)}, u32[]{:S(2)}, u32[]{:S(2)}) collective-permute-start(bf16[1920,384]{1,0:T(8,128)(2,1)} %get-tuple-element.165), channel_id=1, source_target_pairs={{0,4},{4,0},{8,12},{12,8},{16,20},{20,16},{24,28},{28,24},{1,5},{5... | collective-permute-start | bytes 4423688 | tf_op jit(solution)/shard_map/ppermute | solution.py:1085
  293.9 29.1 %collective-permute-start.33 = (bf16[1536,384]{1,0:T(8,128)(2,1)}, bf16[1536,384]{1,0:T(8,128)(2,1)S(1)}, u32[]{:S(2)}, u32[]{:S(2)}) collective-permute-start(bf16[1536,384]{1,0:T(8,128)(2,1)} %get-tuple-element.187), channel_id=1, source_target_pairs={{0,2},{2,0},{1,3},{3,1},{4,6},{6,4},{5,7},{7,5},{8,10},{10,8},{9,1... | collective-permute-start | bytes 3538952 | tf_op jit(solution)/shard_map/ppermute | solution.py:1085
  294.8 32.3 %collective-permute-start.10 = (bf16[448,768]{1,0:T(8,128)(2,1)}, bf16[448,768]{1,0:T(8,128)(2,1)}, u32[]{:S(2)}, u32[]{:S(2)}) collective-permute-start(bf16[448,768]{1,0:T(8,128)(2,1)} %get-tuple-element.138), channel_id=1, source_target_pairs={{0,1},{1,0},{2,3},{3,2},{4,5},{5,4},{6,7},{7,6},{8,9},{9,8},{10,11... | collective-permute-start | bytes 2064392 | tf_op jit(solution)/shard_map/ppermute | solution.py:1118
  300.0 55.3 %collective-permute-start.12 = (bf16[448,768]{1,0:T(8,128)(2,1)}, bf16[448,768]{1,0:T(8,128)(2,1)}, u32[]{:S(2)}, u32[]{:S(2)}) collective-permute-start(bf16[448,768]{1,0:T(8,128)(2,1)} %add_convert_fusion), channel_id=1, source_target_pairs={{0,2},{2,0},{1,3},{3,1},{4,6},{6,4},{5,7},{7,5},{8,10},{10,8},{9,1... | collective-permute-start | bytes 2064392 | tf_op jit(solution)/shard_map/ppermute | solution.py:1119
  310.7 42.1 %collective-permute-start.28 = (bf16[640,384]{1,0:T(8,128)(2,1)}, bf16[640,384]{1,0:T(8,128)(2,1)}, u32[]{:S(2)}, u32[]{:S(2)}) collective-permute-start(bf16[640,384]{1,0:T(8,128)(2,1)} %get-tuple-element.179), channel_id=1, source_target_pairs={{0,4},{4,0},{8,12},{12,8},{16,20},{20,16},{24,28},{28,24},{1,5},{5... | collective-permute-start | bytes 1474568 | tf_op jit(solution)/shard_map/ppermute | solution.py:1085
  323.0 44.3 %collective-permute-start.17 = (bf16[768,384]{1,0:T(8,128)(2,1)}, bf16[768,384]{1,0:T(8,128)(2,1)}, u32[]{:S(2)}, u32[]{:S(2)}) collective-permute-start(bf16[768,384]{1,0:T(8,128)(2,1)} %get-tuple-element.153), channel_id=1, source_target_pairs={{0,8},{4,12},{8,0},{12,4},{16,24},{20,28},{24,16},{28,20},{1,9},{5... | collective-permute-start | bytes 1769480 | tf_op jit(solution)/shard_map/ppermute | solution.py:1085
  327.1 42.7 %collective-permute-start.34 = (bf16[768,384]{1,0:T(8,128)(2,1)}, bf16[768,384]{1,0:T(8,128)(2,1)}, u32[]{:S(2)}, u32[]{:S(2)}) collective-permute-start(bf16[768,384]{1,0:T(8,128)(2,1)} %get-tuple-element.189), channel_id=1, source_target_pairs={{0,4},{4,0},{8,12},{12,8},{16,20},{20,16},{24,28},{28,24},{1,5},{5... | collective-permute-start | bytes 1769480 | tf_op jit(solution)/shard_map/ppermute | solution.py:1085
  342.3 31.2 %collective-permute-start.14 = (bf16[384,768]{1,0:T(8,128)(2,1)}, bf16[384,768]{1,0:T(8,128)(2,1)}, u32[]{:S(2)}, u32[]{:S(2)}) collective-permute-start(bf16[384,768]{1,0:T(8,128)(2,1)} %fusion.2), channel_id=1, source_target_pairs={{0,2},{2,0},{1,3},{3,1},{4,6},{6,4},{5,7},{7,5},{8,10},{10,8},{9,1... | collective-permute-start | bytes 1769480 | tf_op jit(solution)/shard_map/ppermute | solution.py:1119
  352.8 38.8 %collective-permute-start.22 = (bf16[960,384]{1,0:T(8,128)(2,1)}, bf16[960,384]{1,0:T(8,128)(2,1)S(1)}, u32[]{:S(2)}, u32[]{:S(2)}) collective-permute-start(bf16[960,384]{1,0:T(8,128)(2,1)} %get-tuple-element.167), channel_id=1, source_target_pairs={{0,2},{2,0},{1,3},{3,1},{4,6},{6,4},{5,7},{7,5},{8,10},{10,8},{9,1... | collective-permute-start | bytes 2211848 | tf_op jit(solution)/shard_map/ppermute | solution.py:1085
  364.7 32.3 %collective-permute-start.30 = (bf16[160,384]{1,0:T(8,128)(2,1)}, bf16[160,384]{1,0:T(8,128)(2,1)S(1)}, u32[]{:S(2)}, u32[]{:S(2)}) collective-permute-start(bf16[160,384]{1,0:T(8,128)(2,1)} %get-tuple-element.183), channel_id=1, source_target_pairs={{0,16},{4,20},{8,24},{12,28},{16,0},{20,4},{24,8},{28,12},{1,17},{... | collective-permute-start | bytes 368648 | tf_op jit(solution)/shard_map/ppermute | solution.py:1085
  369.4 27.6 %collective-permute-start.18 = (bf16[384,384]{1,0:T(8,128)(2,1)}, bf16[384,384]{1,0:T(8,128)(2,1)S(1)}, u32[]{:S(2)}, u32[]{:S(2)}) collective-permute-start(bf16[384,384]{1,0:T(8,128)(2,1)} %get-tuple-element.155), channel_id=1, source_target_pairs={{0,16},{4,20},{8,24},{12,28},{16,0},{20,4},{24,8},{28,12},{1,17},{... | collective-permute-start | bytes 884744 | tf_op jit(solution)/shard_map/ppermute | solution.py:1085
  (41 other events, 256.1 us)
